TPU v7x, 256 devices: a whole 4x4x8 slice. The times are simulated.
256 devices in a mesh: chrom: 4 (over z_hi), tile: 32 (over y, x, z_lo), var: 2 (over core).
Axes of the slice: x: 4, y: 4, z: 8 (z_hi: 4, z_lo: 2; z = z_hi * 2 + z_lo), core: 2. Of those that a mesh axis runs over, the one named last changes fastest.
Arguments:
- row_geno: int32 [12288, 2048], P('tile', ('chrom', 'var')), may hold values from 0 to 2, as said below
- col_geno: int32 [4096, 2048], P(('tile', 'var'), 'chrom'), may hold values from 0 to 2, as said below
- allele_freq: float32 [2048], P(('chrom', 'var')), may hold values from 0.05000305 to 0.5, as said below
- snp_counts: int32 [8], replicated, may hold values from 1 to 512, 2048 in all
- group_of: int32 [8], replicated, may hold values from 0 to 3, as said below
- pair_mask: int32 [8, 8], replicated, may hold values 0 or 1
- probes: bfloat16 [4096, 128], P(('tile', 'var')), may hold values from -6 to 6
Outputs:
- kernel_out: bfloat16 [4, 12288, 128], P('chrom', 'tile')
Inputs may be any that keep to these rules, and one draw needn't show every extreme that they name: `group_of`: every group holds at most 4 chromosomes, and some group holds exactly 4. `pair_mask`: the diagonal is not used. `snp_counts`: the counts sum to 2048; the largest is 512. `allele_freq`: multiples of 1 / 65536. `row_geno`: each code is the number of base alleles among two drawn independently, each with the probability allele_freq of its variant. `col_geno`: each code is the number of base alleles among two drawn independently, each with the probability allele_freq of its variant.
All inputs are finite; a program needn't handle non-finite values.
Results may differ from a plain program's by a relative error of at most 0.019.
Values may be sent and summed in bfloat16 or wider, within the bound.
No kernel may reach another device: no remote copies, remote signals or barrier semaphores. Data moves between devices by JAX's collectives and lax.ppermute only.
A program may use at most 64 MiB of HBM per device.

v0:
```python
import jax
import jax.numpy as jnp
from jax import lax
from jax.sharding import PartitionSpec as P

MOST_SNP = 512


def in_one_piece(arrays, axis, dim, along):
    widths = [a.shape[along] for a in arrays]
    both = jnp.concatenate(arrays, axis=along)
    out = lax.all_gather(both, axis, axis=dim, tiled=True)
    return tuple(jnp.split(out, [sum(widths[:k]) for k in range(1, len(widths))], axis=along))


def in_blocks(shard, dim, devices):
    dims = shard.shape
    pieces = shard.reshape(*dims[:dim], devices, dims[dim] // devices, *dims[dim + 1 :])
    return jnp.moveaxis(pieces, dim, 0)


def summed_on_arrival(shard, axis, dim):
    devices = lax.axis_size(axis)
    pieces = lax.all_to_all(in_blocks(shard, dim, devices), axis, 0, 0, tiled=True)
    return jnp.sum(pieces.astype(jnp.float32), axis=0)


def copy_for_each(shard, axis):
    copies = jnp.broadcast_to(shard, (lax.axis_size(axis), *shard.shape))
    return lax.all_to_all(copies, axis, split_axis=0, concat_axis=0, tiled=True)


def of_everyone(shard, axis):
    everything = copy_for_each(shard, axis)
    return jnp.sum(everything.astype(jnp.float32), axis=0)


def variant_tables(frequency, snp_counts, pair_mask):
    variants = frequency.shape[0]
    chromosomes = snp_counts.shape[0]
    ends = jnp.cumsum(snp_counts, dtype=jnp.int32)
    position = jnp.arange(variants, dtype=jnp.int32)
    chrom_of = jnp.sum(
        (position[None, :] >= ends[:, None]).astype(jnp.int32), axis=0, dtype=jnp.int32
    )
    labels = jnp.arange(chromosomes, dtype=jnp.int32)
    members = (chrom_of[None, :] == labels[:, None]).astype(jnp.float32)
    spread_term = 2.0 * frequency * (1.0 - frequency)
    denominator = jnp.dot(members, spread_term)
    own_table = members / denominator[:, None]
    offdiag = pair_mask.astype(jnp.float32) * (1.0 - jnp.eye(chromosomes, dtype=jnp.float32))
    return (own_table, offdiag)


def window_cut(matrix, starts, width):

    def one_cut(start):
        return lax.dynamic_slice_in_dim(matrix, start, width, matrix.ndim - 1)

    return jax.vmap(one_cut)(starts)


def kernel_every(weighted, starts, cols_piece, probe_piece, offdiag):
    cut_cols = window_cut(cols_piece, starts, weighted.shape[2])
    kin_all = jnp.einsum("crm,cnm->crn", weighted, cut_cols, preferred_element_type=jnp.float32)
    partner = jnp.einsum("sc,crn->srn", offdiag, kin_all)
    product = (kin_all * partner).astype(jnp.bfloat16)
    return jnp.einsum("srn,np->srp", product, probe_piece, preferred_element_type=jnp.float32)


def body(row_geno, col_geno, allele_freq, snp_counts, group_of, pair_mask, probes):
    chrom_index = lax.axis_index("chrom")
    local_z = (row_geno.astype(jnp.float32) - 2.0 * allele_freq[None, :]).astype(jnp.bfloat16)
    rows_z, frequency = (
        lax.all_gather(local_z, ("chrom", "var"), axis=1, tiled=True),
        lax.all_gather(
            allele_freq.astype(jnp.bfloat16), ("chrom", "var"), axis=0, tiled=True
        ).astype(allele_freq.dtype),
    )
    group_width = col_geno.shape[1]
    freq_block = lax.dynamic_slice_in_dim(frequency, chrom_index * group_width, group_width)
    local_cols = (col_geno.astype(jnp.float32) - 2.0 * freq_block[None, :]).astype(jnp.bfloat16)
    own_table, offdiag = variant_tables(frequency, snp_counts, pair_mask)
    chromosomes = snp_counts.shape[0]
    variants = frequency.shape[0]
    window = MOST_SNP
    ends = jnp.cumsum(snp_counts, dtype=jnp.int32)
    starts = jnp.clip(ends - snp_counts, 0, variants - window)
    cut_rows = window_cut(rows_z, starts, window).astype(jnp.float32)
    cut_weights = window_cut(own_table, starts, window)
    row_labels = jnp.arange(chromosomes, dtype=jnp.int32)
    own_cut = jnp.sum(
        cut_weights * (row_labels[:, None, None] == row_labels[None, :, None]).astype(jnp.float32),
        axis=1,
    )
    weighted = (cut_rows * own_cut[:, None, :]).astype(jnp.bfloat16)
    groups = lax.axis_size("chrom")
    group_hot = (group_of[:, None] == jnp.arange(groups, dtype=jnp.int32)[None, :]).astype(
        jnp.float32
    )
    quarter = col_geno.shape[0] // groups
    swapped = lax.all_to_all(local_cols, "chrom", split_axis=0, concat_axis=1, tiled=True)
    probe_part = lax.dynamic_slice_in_dim(probes, chrom_index * quarter, quarter, 0)
    pieces = in_one_piece((swapped, probe_part), "tile", 0, 1)
    applied = kernel_every(weighted, starts, pieces[0], pieces[1], offdiag)
    spread_parts = jnp.einsum("sg,srp->grp", group_hot, applied)
    part_sum = summed_on_arrival(spread_parts.astype(jnp.bfloat16), "chrom", 0)
    total = of_everyone(part_sum.astype(jnp.bfloat16), "var").astype(jnp.float32)
    return total.astype(jnp.bfloat16)


def solution(mesh):
    in_specs = (
        P("tile", ("chrom", "var")),
        P(("tile", "var"), "chrom"),
        P(("chrom", "var")),
        P(),
        P(),
        P(),
        P(("tile", "var"), None),
    )
    out_specs = P("chrom", "tile", None)
    return jax.shard_map(body, mesh=mesh, in_specs=in_specs, out_specs=out_specs, check_vma=False)
```

profile of v0, /device:TPU:1, one launch (start us, length us, event | category | flops | bytes accessed | tf_op | source)
XLA Modules:
  0.0 277.2 jit_solution(6447411538022992068)
XLA Ops:
  7.3 1.7 subtract_convert_fusion
  9.0 16.3 %all-gather = bf16[8,1,256]{2,1,0:T(2,128)(2,1)S(1)} all-gather(bf16[1,1,256]{2,1,0:T(2,128)(2,1)S(1)} %reshape.117), channel_id=1, replica_groups=mesh['chrom'=4,'tile'=32,'var'=2] {'chrom','var'}, dimensions={0}, use_global_device_ids=true | all-gather | bytes 4608 | tf_op jit(solution)/shard_map/all_gather | solution.py:76
  27.0 3.3 %all-to-all-start = ((bf16[4,16,512]{2,1,0:T(8,128)(2,1)}), bf16[4,16,512]{2,1,0:T(8,128)(2,1)S(1)}, u32[]{:S(2)}, u32[]{:S(2)}) async-start(bf16[4,16,512]{2,1,0:T(8,128)(2,1)} %bitcast.7), calls=%async_computation | async-start | bytes 131072 | tf_op jit(solution)/shard_map/all_to_all | solution.py:102
  32.1 5.3 %all-to-all-done = bf16[4,16,512]{2,1,0:T(8,128)(2,1)S(1)} async-done(((bf16[4,16,512]{2,1,0:T(8,128)(2,1)}), bf16[4,16,512]{2,1,0:T(8,128)(2,1)S(1)}, u32[]{:S(2)}, u32[]{:S(2)}) %all-to-all-start) | async-done | bytes 65568 | tf_op jit(solution)/shard_map/all_to_all | solution.py:102
  38.2 10.6 %while.4 = (s32[]{:T(128)}, f32[8,2048]{1,0:T(8,128)S(1)}, s32[8,2]{0,1:T(2,128)S(1)}, f32[8,8,512]{2,1,0:T(8,128)S(1)}, s32[]{:T(128)}) while((s32[]{:T(128)}, f32[8,2048]{1,0:T(8,128)S(1)}, s32[8,2]{0,1:T(2,128)S(1)}, f32[8,8,512]{2,1,0:T(8,128)S(1)}, s32[]{:T(128)}) %tuple.45), condition=%wide.while_cond.1, body=%wide.while_body.1.sunk | while | flops 2 | bytes 32873 | solution.py:58
  48.9 1.6 all-gather.4.cloned.1.call-done
  50.5 24.9 %while.3 = (s32[]{:T(128)}, bf16[384,2048]{1,0:T(8,128)(2,1)}, s32[8,2]{0,1:T(2,128)S(1)}, bf16[8,384,512]{2,1,0:T(8,128)(2,1)}, s32[]{:T(128)}) while((s32[]{:T(128)}, bf16[384,2048]{1,0:T(8,128)(2,1)}, s32[8,2]{0,1:T(2,128)S(1)}, bf16[8,384,512]{2,1,0:T(8,128)(2,1)}, s32[]{:T(128)}) %tuple.53), condition=%wide.while_cond, body=%wide.while_body.sunk | while | flops 2 | bytes 787045 | solution.py:58
  51.1 2.5 bitcast_dynamic-update-slice_fusion.6
  54.2 2.5 bitcast_dynamic-update-slice_fusion.6
  57.3 2.5 bitcast_dynamic-update-slice_fusion.6
  60.4 2.6 bitcast_dynamic-update-slice_fusion.6
  63.6 2.5 bitcast_dynamic-update-slice_fusion.6
  66.7 2.5 bitcast_dynamic-update-slice_fusion.6
  69.8 2.5 bitcast_dynamic-update-slice_fusion.6
  73.0 2.5 bitcast_dynamic-update-slice_fusion.6
  75.5 114.9 %all-gather.6.cloned.1.call-done = bf16[512,2176]{1,0:T(8,128)(2,1)} async-done(((bf16[16,2176]{1,0:T(8,128)(2,1)}), bf16[512,2176]{1,0:T(8,128)(2,1)}) %all-gather.6.cloned.1.call-update) | async-done | bytes 2228240 | tf_op jit(solution)/shard_map/all_gather | solution.py:12
  190.4 1.6 slice-done
  192.0 18.7 %while.5 = (s32[]{:T(128)}, bf16[512,2048]{1,0:T(8,128)(2,1)S(1)}, s32[8,2]{0,1:T(2,128)S(1)}, bf16[8,512,512]{2,1,0:T(8,128)(2,1)}, s32[]{:T(128)}) while((s32[]{:T(128)}, bf16[512,2048]{1,0:T(8,128)(2,1)S(1)}, s32[8,2]{0,1:T(2,128)S(1)}, bf16[8,512,512]{2,1,0:T(8,128)(2,1)}, s32[]{:T(128)}) %tuple.54), condition=%wide.while_cond.2, body=%wide.while_body.2.sunk | while | flops 2 | bytes 1049189 | solution.py:58
  192.6 1.7 bitcast_dynamic-update-slice_fusion.8
  194.9 1.7 bitcast_dynamic-update-slice_fusion.8
  197.2 1.8 bitcast_dynamic-update-slice_fusion.8
  199.6 1.7 bitcast_dynamic-update-slice_fusion.8
  201.9 1.8 bitcast_dynamic-update-slice_fusion.8
  204.3 1.8 bitcast_dynamic-update-slice_fusion.8
  206.6 1.7 bitcast_dynamic-update-slice_fusion.8
  208.9 1.7 bitcast_dynamic-update-slice_fusion.8
  210.7 5.0 %fusion.3 = f32[8,384,512]{2,1,0:T(8,128)S(1)} fusion(bf16[8,512,512]{2,1,0:T(8,128)(2,1)} %get-tuple-element.28, bf16[8,384,512]{2,1,0:T(8,128)(2,1)} %get-tuple-element.12, f32[8,512]{1,0:T(8,128)S(1)} %multiply_reduce_fusion), kind=kOutput, calls=%fused_computation.11 | convolution fusion | flops 1615331328 | bytes 13647872 | tf_op jit(solution)/shard_map/crm,cnm->crn/dot_general | solution.py:65
  215.7 3.6 %fusion.1 = f32[8,384,512]{2,0,1:T(8,128)S(1)} fusion(f32[8,384,512]{2,1,0:T(8,128)S(1)} %fusion.3, s32[8,8]{1,0:T(8,128)S(1)} %copy-done.2), kind=kOutput, calls=%fused_computation.8 | convolution fusion | flops 25166144 | bytes 12583168 | tf_op jit(solution)/shard_map/sc,crn->srn/dot_general | solution.py:66
  219.3 5.3 %fusion = bf16[8,384,512]{2,1,0:T(8,128)(2,1)} fusion(f32[8,384,512]{2,1,0:T(8,128)S(1)} %fusion.3, f32[8,384,512]{2,0,1:T(8,128)S(1)} %fusion.1), kind=kLoop, calls=%fused_computation.7 | loop fusion | flops 3145728 | bytes 15728640 | tf_op jit(solution)/shard_map/convert_element_type | solution.py:67
  224.6 4.0 %fusion.13 = bf16[4,1,384,128]{3,0,2,1:T(4,128)(2,1)S(1)} fusion(bf16[8,384,512]{2,1,0:T(8,128)(2,1)} %fusion, bf16[512,2176]{1,0:T(8,128)(2,1)S(1)} %copy-done.1, s32[8]{0:T(128)S(1)} %copy-done.3), kind=kOutput, calls=%fused_computation.17 | convolution fusion | flops 405995552 | bytes 3670528 | tf_op jit(solution)/shard_map/sg,srp->grp/dot_general | solution.py:106
  228.7 15.7 %all_to_all.29 = bf16[4,1,384,128]{3,2,1,0:T(8,128)(2,1)S(1)} all-to-all(bf16[4,1,384,128]{3,2,1,0:T(8,128)(2,1)S(1)} %copy.19), channel_id=1, replica_groups=mesh['chrom'=4,'tile'=32,'var'=2] {'chrom'}, dimensions={0} | all-to-all | bytes 786432 | tf_op jit(solution)/shard_map/all_to_all | solution.py:24
  244.5 25.1 %all_to_all.30 = bf16[2,1,384,128]{3,2,1,0:T(8,128)(2,1)S(1)} all-to-all(bf16[2,1,384,128]{3,2,1,0:T(8,128)(2,1)S(1)} %broadcast_in_dim.5), channel_id=1, replica_groups=mesh['chrom'=4,'tile'=32,'var'=2] {'var'}, dimensions={0} | all-to-all | bytes 393216 | tf_op jit(solution)/shard_map/all_to_all | solution.py:30
  (93 shorter events, 25.8 us)
Async XLA Ops:
  6.5 25.6 %copy-start = (bf16[64,128]{1,0:T(8,128)(2,1)S(1)}, bf16[64,128]{1,0:T(8,128)(2,1)}, u32[]{:S(2)}) copy-start(bf16[64,128]{1,0:T(8,128)(2,1)} %param.13) | copy-start | bytes 49156
  6.5 44.0 %all-gather.4.cloned.1.call-start = ((), (), s32[]{:S(2)}) async-start(), calls=%async_computation.3 | async-start | bytes 1769472 | tf_op jit(solution)/shard_map/all_gather | solution.py:75
  27.0 10.4 %all-to-all-start = ((bf16[4,16,512]{2,1,0:T(8,128)(2,1)}), bf16[4,16,512]{2,1,0:T(8,128)(2,1)S(1)}, u32[]{:S(2)}, u32[]{:S(2)}) async-start(bf16[4,16,512]{2,1,0:T(8,128)(2,1)} %bitcast.7), calls=%async_computation | async-start | bytes 131072 | tf_op jit(solution)/shard_map/all_to_all | solution.py:102
  30.3 160.0 %all-gather.6.cloned.1.call-start = ((), (), s32[]{:S(2)}) async-start(), calls=%async_computation.4 | async-start | bytes 2297856 | tf_op jit(solution)/shard_map/all_gather | solution.py:12
  190.4 1.6 slice-start
  210.7 5.0 %copy-start.2 = (s32[8,8]{1,0:T(8,128)S(1)}, s32[8,8]{1,0:T(8,128)}, u32[]{:S(2)}) copy-start(s32[8,8]{1,0:T(8,128)} %param.12) | copy-start | bytes 772
  219.3 5.3 %copy-start.1 = (bf16[512,2176]{1,0:T(8,128)(2,1)S(1)}, bf16[512,2176]{1,0:T(8,128)(2,1)}, u32[]{:S(2)}) copy-start(bf16[512,2176]{1,0:T(8,128)(2,1)} %all-gather.6.cloned.1.call-done) | copy-start | bytes 6684676
  219.3 5.3 %copy-start.3 = (s32[8]{0:T(128)S(1)}, s32[8]{0:T(128)}, u32[]{:S(2)}) copy-start(s32[8]{0:T(128)} %param.11) | copy-start | bytes 100
Sparse Core Ops, SparseCore 0:
  9.2 41.3 all-gather.3
  52.3 138.0 all-gather.5
where the time goes:
time: 278 us; the launch traced here: 277 us
  waiting for transfers between devices  122 us (44%)
  blocking collectives  57.2 us (21%)
  local copies, waits for them, and re-layouts  55.9 us (20%)
  between operations  13.5 us (5%)
  matrix products  12.8 us (5%)
  other arithmetic  12.6 us (5%)
  starting transfers between devices  3.34 us (1%)
    all_gather x1, waiting for transfers between devices, in_one_piece(): out = lax.all_gather(both, axis, axis=dim, tiled=True)  115 us
    gather x72, local copies, waits for them, and re-layouts  54.2 us
    all_to_all x1, blocking collectives, copy_for_each(): return lax.all_to_all(copies, axis, split_axis=0, concat_axis=0, tiled=True)  25.1 us
    all_gather x1, blocking collectives, body(): lax.all_gather(allele_freq.astype(jnp.bfloat16), ('chrom', 'var'), axis=0...  16.3 us
    all_to_all x1, blocking collectives, summed_on_arrival(): lax.all_to_all(in_blocks(shard, dim, devices), axis, 0, 0, tiled=True)  15.7 us
  transfers between devices with their start and end apart: 3, of which 3 were waited for; matrix products, arithmetic and copies ran while one was open for 14% of the time, Pallas kernels for 0%

commit v1 on v0

v1 whole, which is shorter than its diff:
```python
import jax
import jax.numpy as jnp
from jax import lax
from jax.experimental import pallas as pl
from jax.experimental.pallas import tpu as pltpu
from jax.sharding import Mesh, PartitionSpec as P

MOST_SNP = 512
LANES = 128
WINDOW = MOST_SNP + LANES
BF16, F32 = jnp.bfloat16, jnp.float32
NT = (((1,), (1,)), ((), ()))


def segments(counts_ref, variants):
    out, first = [], jnp.int32(0)
    for a in range(counts_ref.shape[0]):
        end = first + counts_ref[a]
        start = jnp.minimum(first // LANES, (variants - WINDOW) // LANES) * LANES
        out.append((first, end, pl.multiple_of(start, LANES)))
        first = end
    return out


def apply_kernel(
    me_ref, counts_ref, group_ref, mask_ref, own_hbm, other_hbm, cols_hbm, *refs
):
    out_refs = refs[: -9]
    cols_ref, rows_ref, tail_ref, z_ref, kin_ref, had_ref, sum_ref, row_sem, col_sem = refs[-9:]
    rows, variants = rows_ref.shape
    columns = z_ref.shape[0]
    blocks, each, _ = cols_ref.shape
    pieces, _, block = own_hbm.shape
    chromosomes, groups = counts_ref.shape[0], sum_ref.shape[0]
    fetch = pltpu.make_async_copy(cols_hbm, cols_ref, col_sem)
    copies = []
    for h, hbm in enumerate((own_hbm, other_hbm)):
        half = me_ref[1] if h == 0 else 1 - me_ref[1]
        for k in range(pieces):
            spot = pl.ds(pl.multiple_of((2 * k + half) * block, block), block)
            copies.append((hbm.at[k, rows : rows + 16, :], tail_ref.at[:, spot]))
            copies.append((hbm.at[k, 0:rows, :], rows_ref.at[:, spot]))
    copies = [
        pltpu.make_async_copy(source, target, row_sem.at[i])
        for i, (source, target) in enumerate(copies)
    ]
    for copy in copies:
        copy.start()
    fetch.start()
    for copy in copies:
        copy.wait()
    tail = tail_ref[...].astype(F32)
    twice = 2.0 * (tail[0:1] + tail[1:2])
    spread = twice * (1.0 - 0.5 * twice)
    lane = lax.broadcasted_iota(jnp.int32, (1, variants), 1)
    fetch.wait()
    for k in range(blocks):
        codes = cols_ref[k, :, 0:variants].astype(F32)
        z_ref[k * each : (k + 1) * each, :] = (codes - twice).astype(BF16)
    for a, (first, end, start) in enumerate(segments(counts_ref, variants)):
        member = (lane >= first) & (lane < end)
        denominator = jnp.sum(jnp.where(member, spread, 0.0), axis=1, keepdims=True)
        here = start + lax.broadcasted_iota(jnp.int32, (1, WINDOW), 1)
        own = jnp.where((here >= first) & (here < end), 1.0 / denominator, 0.0)
        window = rows_ref[:, pl.ds(start, WINDOW)].astype(F32)
        weighted = (window * own).astype(BF16)
        kin_ref[a] = lax.dot_general(
            weighted, z_ref[:, pl.ds(start, WINDOW)], NT, preferred_element_type=F32
        )
    pairs = [[mask_ref[a, b].astype(F32) for b in range(chromosomes)] for a in range(chromosomes)]
    high = 16

    @pl.loop(0, rows // high)
    def _(i):
        at = pl.ds(pl.multiple_of(i * high, high), high)
        for n in range(0, columns, LANES):
            kin = [kin_ref[b, at, n : n + LANES] for b in range(chromosomes)]
            for a in range(chromosomes):
                partner = None
                for b in range(chromosomes):
                    if b != a:
                        term = pairs[a][b] * kin[b]
                        partner = term if partner is None else partner + term
                had_ref[a, at, n : n + LANES] = (kin[a] * partner).astype(BF16)

    sum_ref[...] = jnp.zeros_like(sum_ref)
    probes = cols_ref[:, :, variants:].reshape(columns, -1)
    for a in range(chromosomes):
        sum_ref[group_ref[a]] += jnp.dot(had_ref[a], probes, preferred_element_type=F32)
    for k, out_ref in enumerate(out_refs):
        out_ref[...] = sum_ref[lax.rem(me_ref[0] + k, groups)].astype(BF16)


def apply(me, own, other, cols, snp_counts, group_of, pair_mask, groups):
    pieces, padded, block = own.shape
    rows, variants = padded - 16, 2 * pieces * block
    columns, samples = cols.shape[0] * cols.shape[1], cols.shape[2] - variants
    chromosomes = snp_counts.shape[0]
    smem = pl.BlockSpec(memory_space=pltpu.SMEM)
    vmem = pl.BlockSpec(memory_space=pltpu.VMEM)
    return pl.pallas_call(
        apply_kernel,
        out_shape=[jax.ShapeDtypeStruct((rows, samples), BF16)] * groups,
        in_specs=[smem] * 4 + [pl.BlockSpec(memory_space=pl.ANY)] * 3,
        out_specs=[vmem] * groups,
        scratch_shapes=[
            pltpu.VMEM(cols.shape, BF16),
            pltpu.VMEM((rows, variants), BF16),
            pltpu.VMEM((16, variants), BF16),
            pltpu.VMEM((columns, variants), BF16),
            pltpu.VMEM((chromosomes, rows, columns), F32),
            pltpu.VMEM((chromosomes, rows, columns), BF16),
            pltpu.VMEM((groups, rows, samples), F32),
            pltpu.SemaphoreType.DMA((4 * pieces,)),
            pltpu.SemaphoreType.DMA,
        ],
        compiler_params=pltpu.CompilerParams(vmem_limit_bytes=30 << 20),
        name="apply",
    )(me, snp_counts, group_of, pair_mask, own, other, cols)


def shifted(x, axis, k):
    n = lax.axis_size(axis)
    return lax.ppermute(x, axis, [(i, (i + k) % n) for i in range(n)])


def body(row_geno, col_geno, allele_freq, snp_counts, group_of, pair_mask, probes):
    groups, lows = lax.axis_size("c"), lax.axis_size("l")
    c, v = lax.axis_index("c"), lax.axis_index("v")
    columns, width = col_geno.shape
    quarter = columns // groups

    codes = jnp.concatenate([col_geno.astype(BF16), probes], axis=1)
    codes = jnp.broadcast_to(
        codes.reshape(groups, 1, quarter, codes.shape[1]), (groups, lows, quarter, codes.shape[1])
    ).reshape(groups * lows, quarter, -1)
    mine = lax.all_to_all(codes, ("c", "l"), 0, 0, tiled=True)
    mine = mine.reshape(groups, lows, quarter, -1)
    held = jnp.concatenate(
        [mine[k, :, :, :width] for k in range(groups)] + [mine[0, :, :, width:]], axis=-1
    ).reshape(lows * quarter, -1)
    plane = lax.axis_size("y") * lax.axis_size("x")
    cols = lax.all_to_all(
        jnp.broadcast_to(held[None], (plane, *held.shape)), ("y", "x"), 0, 0, tiled=True
    )

    coarse = lax.reduce_precision(allele_freq, 8, 7)
    fine = allele_freq - coarse
    tail = jnp.concatenate(
        [coarse[None], fine[None], jnp.zeros((14, allele_freq.shape[0]), F32)], axis=0
    ).astype(BF16)
    local = jnp.concatenate(
        [(row_geno.astype(F32) - 2.0 * allele_freq[None, :]).astype(BF16), tail], axis=0
    )
    own = lax.all_gather(local, "c", axis=0, tiled=False)
    other = shifted(own, "v", 1)
    me = jnp.stack([c, v]).astype(jnp.int32)
    parts = apply(me, own, other, cols, snp_counts, group_of, pair_mask, groups)

    sums = parts[0].astype(F32)
    for k in (2, 1, 3):
        sums = sums + shifted(parts[k], "c", k).astype(F32)
    total = sums.astype(BF16)
    across = shifted(total, "v", 1)
    return (total.astype(F32) + across.astype(F32)).astype(BF16)[None]


def solution(mesh):
    chrom, tile, var = (mesh.shape[k] for k in ("chrom", "tile", "var"))
    fine = Mesh(mesh.devices.reshape(chrom, 4, 4, tile // 16, var), ("c", "y", "x", "l", "v"))
    tile_axes = ("y", "x", "l")
    in_specs = (
        P(tile_axes, ("c", "v")),
        P((*tile_axes, "v"), "c"),
        P(("c", "v")),
        P(),
        P(),
        P(),
        P((*tile_axes, "v"), None),
    )
    out_specs = P("c", tile_axes, None)
    return jax.shard_map(body, mesh=fine, in_specs=in_specs, out_specs=out_specs, check_vma=False)
```

time: 278 us -> 83.4 us (0.30)
  waiting for transfers between devices: 122 us -> 10.8 us
  local copies, waits for them, and re-layouts: 55.9 us -> 1.68 us
  blocking collectives: 57.2 us -> 33.7 us
  starting transfers between devices: 3.34 us -> 24.3 us
  between operations: 13.5 us -> 0.15 us
  matrix products: 12.8 us -> 0 us
  other arithmetic: 12.6 us -> 2.61 us
  Pallas kernels: 0 us -> 9.84 us
    all_gather x2 -> x0, waiting for transfers between devices: 117 us -> none  [the longest x1 115 us: in_one_piece(): out = lax.all_gather(both, axis, axis=dim, tiled=True)]
    gather x72 -> x0, local copies, waits for them, and re-layouts: 54.2 us -> none
    all_to_all x2 -> x1, blocking collectives: 40.8 us -> 17 us  [body(): mine = lax.all_to_all(codes, ('c', 'l'), 0, 0, tiled=True)]
    ppermute x0 -> x5, starting transfers between devices: none -> 17.4 us  [shifted(): return lax.ppermute(x, axis, [(i, (i + k) % n) for i in range(n)])]
    dot_general x4 -> x0, matrix products: 12.8 us -> none  [the longest x1 4.99 us: kernel_every(): jnp.einsum('crm,cnm->crn', weighted, cut_cols, preferred_element_type=jnp...]
    pallas_call x0 -> x1, Pallas kernels: none -> 9.84 us  [apply(): pl.pallas_call(apply_kernel, out_shape=[jax.ShapeDtypeStruct((rows, sampl...]
    ppermute x0 -> x5, waiting for transfers between devices: none -> 8.31 us  [shifted(): return lax.ppermute(x, axis, [(i, (i + k) % n) for i in range(n)])]
    convert_element_type x5 -> x3, other arithmetic: 8.59 us -> 1.01 us  [the longest x1 0.91 us: body(): codes = jnp.concatenate([col_geno.astype(BF16), probes], axis=1)]
  transfers between devices with their start and end apart: 3 -> 6, of which waited for: 3 -> 5; matrix products, arithmetic and copies ran while one was open for 14% -> 0% of each run, Pallas kernels for 0% -> 0%
where the time goes in v1:
time: 83.4 us; the launch traced here: 83.1 us
  blocking collectives  33.7 us (40%)
  starting transfers between devices  24.3 us (29%)
  waiting for transfers between devices  10.8 us (13%)
  Pallas kernels  9.84 us (12%)
  other arithmetic  2.61 us (3%)
  local copies, waits for them, and re-layouts  1.68 us (2%)
    ppermute x5, starting transfers between devices, shifted(): return lax.ppermute(x, axis, [(i, (i + k) % n) for i in range(n)])  17.4 us
    all_to_all x1, blocking collectives, body(): mine = lax.all_to_all(codes, ('c', 'l'), 0, 0, tiled=True)  17 us
    all_gather x1, blocking collectives, body(): own = lax.all_gather(local, 'c', axis=0, tiled=False)  16.7 us
    pallas_call x1, Pallas kernels, apply(): pl.pallas_call(apply_kernel, out_shape=[jax.ShapeDtypeStruct((rows, sampl...  9.84 us
    ppermute x5, waiting for transfers between devices, shifted(): return lax.ppermute(x, axis, [(i, (i + k) % n) for i in range(n)])  8.31 us
    all_to_all x1, starting transfers between devices, body(): lax.all_to_all(jnp.broadcast_to(held[None], (plane, *held.shape)), ('y',...  6.9 us
    all_to_all x1, waiting for transfers between devices, body(): lax.all_to_all(jnp.broadcast_to(held[None], (plane, *held.shape)), ('y',...  2.5 us
  transfers between devices with their start and end apart: 6, of which 5 were waited for; matrix products, arithmetic and copies ran while one was open for 0% of the time, Pallas kernels for 0%

profile of v1, /device:TPU:1, one launch (start us, length us, event | category | flops | bytes accessed | tf_op | source)
XLA Modules:
  0.0 83.1 jit_solution(10945226425590842652)
XLA Ops:
  0.0 0.9 %convert_element_type.36 = bf16[64,512]{1,0:T(8,128)(2,1)S(1)} convert(s32[64,512]{1,0:T(8,128)} %param.8) | non-fusion elementwise | flops 32768 | bytes 196608 | tf_op jit(solution)/shard_map/convert_element_type | solution.py:133
  0.9 0.7 pad_maximum_fusion
  1.7 17.0 %all_to_all.10 = bf16[8,16,640]{2,1,0:T(8,128)(2,1)S(1)} all-to-all(bf16[8,16,640]{2,1,0:T(8,128)(2,1)S(1)} %bitcast.16), channel_id=1, replica_groups=mesh['c'=4,'y'=4,'x'=4,'l'=2,'v'=2] {'c','l'}, dimensions={0} | all-to-all | bytes 327680 | tf_op jit(solution)/shard_map/all_to_all | solution.py:137
  18.7 1.5 %broadcast_in_dim.35 = bf16[16,32,2176]{2,1,0:T(8,128)(2,1)} broadcast(bf16[32,2176]{1,0:T(8,128)(2,1)S(1)} %bitcast.20), dimensions={1,2} | broadcast | bytes 2367488 | tf_op jit(solution)/shard_map/broadcast_in_dim | solution.py:144
  20.2 0.0 copy-start.4
  20.2 0.0 copy-start.3
  20.2 0.0 copy-start
  20.2 0.0 copy-start.2
  20.3 6.9 %all-to-all-start.1 = ((bf16[16,32,2176]{2,1,0:T(8,128)(2,1)}), bf16[16,32,2176]{2,1,0:T(8,128)(2,1)S(1)}, u32[]{:S(2)}, u32[]{:S(2)}) async-start(bf16[16,32,2176]{2,1,0:T(8,128)(2,1)} %broadcast_in_dim.35), calls=%async_computation.1 | async-start | bytes 4456448 | tf_op jit(solution)/shard_map/all_to_all | solution.py:143
  27.2 0.0 copy-done.4
  27.2 0.1 pad.5.clone
  27.3 0.0 copy-done.3
  27.3 0.1 maximum_maximum_fusion
  27.5 16.7 %all-gather = bf16[1600,256]{1,0:T(8,128)(2,1)S(1)} all-gather(bf16[400,256]{1,0:T(8,128)(2,1)S(1)} %maximum_maximum_fusion), channel_id=2, replica_groups=mesh['c'=4,'y'=4,'x'=4,'l'=2,'v'=2] {'c'}, dimensions={0}, use_global_device_ids=true | all-gather | bytes 1024000 | tf_op jit(solution)/shard_map/all_gather | solution.py:155
  44.2 5.1 %collective-permute-start = (bf16[4,400,256]{2,1,0:T(8,128)(2,1)S(1)}, bf16[4,400,256]{2,1,0:T(8,128)(2,1)}, u32[]{:S(2)}, u32[]{:S(2)}) collective-permute-start(bf16[4,400,256]{2,1,0:T(8,128)(2,1)S(1)} %bitcast.14), channel_id=1, source_target_pairs={{0,1},{1,0},{2,3},{3,2},{4,5},{5,4},{6,7},{7,6},{8,9},{9,8},{10,11... | collective-permute-start | bytes 2457608 | tf_op jit(solution)/shard_map/ppermute | solution.py:124
  49.3 0.1 pad_add_fusion.me_ref
  49.4 2.0 %collective-permute-done.other_hbm = bf16[4,400,256]{2,1,0:T(8,128)(2,1)} collective-permute-done((bf16[4,400,256]{2,1,0:T(8,128)(2,1)S(1)}, bf16[4,400,256]{2,1,0:T(8,128)(2,1)}, u32[]{:S(2)}, u32[]{:S(2)}) %collective-permute-start) | collective-permute-done | bytes 819232 | tf_op jit(solution)/shard_map/ppermute | solution.py:124
  51.4 2.5 %all-to-all-done.1.cols_hbm = bf16[16,32,2176]{2,1,0:T(8,128)(2,1)S(1)} async-done(((bf16[16,32,2176]{2,1,0:T(8,128)(2,1)}), bf16[16,32,2176]{2,1,0:T(8,128)(2,1)S(1)}, u32[]{:S(2)}, u32[]{:S(2)}) %all-to-all-start.1) | async-done | bytes 2228256 | tf_op jit(solution)/shard_map/all_to_all | solution.py:143
  53.9 0.0 copy-done
  53.9 0.0 copy-done.1
  53.9 0.0 copy-done.2
  53.9 9.8 %apply.1 = (bf16[384,128]{1,0:T(8,128)(2,1)S(1)}, bf16[384,128]{1,0:T(8,128)(2,1)S(1)}, bf16[384,128]{1,0:T(8,128)(2,1)S(1)}, bf16[384,128]{1,0:T(8,128)(2,1)S(1)}) custom-call(s32[2]{0:T(128)S(1)} %pad_add_fusion.me_ref, s32[8]{0:T(128)S(1)} %copy-done.1, s32[8]{0:T(128)S(1)} %copy-done.2, s32[8,8]{1,0:T(8,128)S(1)} %copy-done, ...), custom_call_target="tpu_custom_call" | custom-call | tf_op jit(solution)/shard_map/apply/pallas_call | solution.py:101
  63.7 2.6 %collective-permute-start.1 = (bf16[384,128]{1,0:T(8,128)(2,1)S(1)}, bf16[384,128]{1,0:T(8,128)(2,1)S(1)}, u32[]{:S(2)}, u32[]{:S(2)}) collective-permute-start(bf16[384,128]{1,0:T(8,128)(2,1)S(1)} %get-tuple-element.10), channel_id=1, source_target_pairs={{0,128},{64,192},{128,0},{192,64},{1,129},{65,193},{129,1},{193,65... | collective-permute-start | bytes 294920 | tf_op jit(solution)/shard_map/ppermute | solution.py:124
  66.3 5.0 %collective-permute-start.2 = (bf16[384,128]{1,0:T(8,128)(2,1)S(1)}, bf16[384,128]{1,0:T(8,128)(2,1)S(1)}, u32[]{:S(2)}, u32[]{:S(2)}) collective-permute-start(bf16[384,128]{1,0:T(8,128)(2,1)S(1)} %get-tuple-element.11), channel_id=1, source_target_pairs={{0,64},{64,128},{128,192},{192,0},{1,65},{65,129},{129,193},{193,1... | collective-permute-start | bytes 294920 | tf_op jit(solution)/shard_map/ppermute | solution.py:124
  71.3 0.0 collective-permute-start.3
  71.3 0.1 collective-permute-done.1
  71.4 5.2 %collective-permute-done.2 = bf16[384,128]{1,0:T(8,128)(2,1)S(1)} collective-permute-done((bf16[384,128]{1,0:T(8,128)(2,1)S(1)}, bf16[384,128]{1,0:T(8,128)(2,1)S(1)}, u32[]{:S(2)}, u32[]{:S(2)}) %collective-permute-start.2) | collective-permute-done | bytes 98336 | tf_op jit(solution)/shard_map/ppermute | solution.py:124
  76.6 0.0 collective-permute-done.3
  76.7 0.1 add_convert_fusion.1
  76.7 4.7 %collective-permute-start.4 = (bf16[384,128]{1,0:T(8,128)(2,1)S(1)}, bf16[384,128]{1,0:T(8,128)(2,1)S(1)}, u32[]{:S(2)}, u32[]{:S(2)}) collective-permute-start(bf16[384,128]{1,0:T(8,128)(2,1)S(1)} %add_convert_fusion.1), channel_id=1, source_target_pairs={{0,1},{1,0},{2,3},{3,2},{4,5},{5,4},{6,7},{7,6},{8,9},{9,8},{10,11... | collective-permute-start | bytes 294920 | tf_op jit(solution)/shard_map/ppermute | solution.py:124
  81.4 0.9 %collective-permute-done.4 = bf16[384,128]{1,0:T(8,128)(2,1)S(1)} collective-permute-done((bf16[384,128]{1,0:T(8,128)(2,1)S(1)}, bf16[384,128]{1,0:T(8,128)(2,1)S(1)}, u32[]{:S(2)}, u32[]{:S(2)}) %collective-permute-start.4) | collective-permute-done | bytes 98336 | tf_op jit(solution)/shard_map/ppermute | solution.py:124
  82.4 0.7 fusion
  (14 shorter events, 0.1 us)
Async XLA Ops:
  20.2 6.9 %copy-start.4 = (f32[256]{0:T(256)S(1)}, f32[256]{0:T(256)}, u32[]{:S(2)}) copy-start(f32[256]{0:T(256)} %param.9) | copy-start | bytes 3076
  20.2 7.1 %copy-start.3 = (s32[384,256]{1,0:T(8,128)S(1)}, s32[384,256]{1,0:T(8,128)}, u32[]{:S(2)}) copy-start(s32[384,256]{1,0:T(8,128)} %param.7) | copy-start | bytes 1179652
  20.2 33.6 %copy-start = (s32[8,8]{1,0:T(8,128)S(1)}, s32[8,8]{1,0:T(8,128)}, u32[]{:S(2)}) copy-start(s32[8,8]{1,0:T(8,128)} %mask_ref.1) | copy-start | bytes 772
  20.2 33.6 %copy-start.1 = (s32[8]{0:T(128)S(1)}, s32[8]{0:T(128)}, u32[]{:S(2)}) copy-start(s32[8]{0:T(128)} %counts_ref.1) | copy-start | bytes 100
  20.2 33.6 %copy-start.2 = (s32[8]{0:T(128)S(1)}, s32[8]{0:T(128)}, u32[]{:S(2)}) copy-start(s32[8]{0:T(128)} %group_ref.1) | copy-start | bytes 100
  20.3 33.6 %all-to-all-start.1 = ((bf16[16,32,2176]{2,1,0:T(8,128)(2,1)}), bf16[16,32,2176]{2,1,0:T(8,128)(2,1)S(1)}, u32[]{:S(2)}, u32[]{:S(2)}) async-start(bf16[16,32,2176]{2,1,0:T(8,128)(2,1)} %broadcast_in_dim.35), calls=%async_computation.1 | async-start | bytes 4456448 | tf_op jit(solution)/shard_map/all_to_all | solution.py:143
  44.2 7.2 %collective-permute-start = (bf16[4,400,256]{2,1,0:T(8,128)(2,1)S(1)}, bf16[4,400,256]{2,1,0:T(8,128)(2,1)}, u32[]{:S(2)}, u32[]{:S(2)}) collective-permute-start(bf16[4,400,256]{2,1,0:T(8,128)(2,1)S(1)} %bitcast.14), channel_id=1, source_target_pairs={{0,1},{1,0},{2,3},{3,2},{4,5},{5,4},{6,7},{7,6},{8,9},{9,8},{10,11... | collective-permute-start | bytes 2457608 | tf_op jit(solution)/shard_map/ppermute | solution.py:124
  63.7 7.7 %collective-permute-start.1 = (bf16[384,128]{1,0:T(8,128)(2,1)S(1)}, bf16[384,128]{1,0:T(8,128)(2,1)S(1)}, u32[]{:S(2)}, u32[]{:S(2)}) collective-permute-start(bf16[384,128]{1,0:T(8,128)(2,1)S(1)} %get-tuple-element.10), channel_id=1, source_target_pairs={{0,128},{64,192},{128,0},{192,64},{1,129},{65,193},{129,1},{193,65... | collective-permute-start | bytes 294920 | tf_op jit(solution)/shard_map/ppermute | solution.py:124
  66.3 10.3 %collective-permute-start.2 = (bf16[384,128]{1,0:T(8,128)(2,1)S(1)}, bf16[384,128]{1,0:T(8,128)(2,1)S(1)}, u32[]{:S(2)}, u32[]{:S(2)}) collective-permute-start(bf16[384,128]{1,0:T(8,128)(2,1)S(1)} %get-tuple-element.11), channel_id=1, source_target_pairs={{0,64},{64,128},{128,192},{192,0},{1,65},{65,129},{129,193},{193,1... | collective-permute-start | bytes 294920 | tf_op jit(solution)/shard_map/ppermute | solution.py:124
  71.3 5.4 %collective-permute-start.3 = (bf16[384,128]{1,0:T(8,128)(2,1)S(1)}, bf16[384,128]{1,0:T(8,128)(2,1)S(1)}, u32[]{:S(2)}, u32[]{:S(2)}) collective-permute-start(bf16[384,128]{1,0:T(8,128)(2,1)S(1)} %get-tuple-element.12), channel_id=1, source_target_pairs={{0,192},{64,0},{128,64},{192,128},{1,193},{65,1},{129,65},{193,129... | collective-permute-start | bytes 294920 | tf_op jit(solution)/shard_map/ppermute | solution.py:124
  76.7 5.7 %collective-permute-start.4 = (bf16[384,128]{1,0:T(8,128)(2,1)S(1)}, bf16[384,128]{1,0:T(8,128)(2,1)S(1)}, u32[]{:S(2)}, u32[]{:S(2)}) collective-permute-start(bf16[384,128]{1,0:T(8,128)(2,1)S(1)} %add_convert_fusion.1), channel_id=1, source_target_pairs={{0,1},{1,0},{2,3},{3,2},{4,5},{5,4},{6,7},{7,6},{8,9},{9,8},{10,11... | collective-permute-start | bytes 294920 | tf_op jit(solution)/shard_map/ppermute | solution.py:124

commit v2 on v1

--- a/solution.py
+++ b/solution.py
@@ -25,8 +25,7 @@
 def apply_kernel(
     me_ref, counts_ref, group_ref, mask_ref, own_hbm, other_hbm, cols_hbm, *refs
 ):
-    out_refs = refs[: -9]
-    cols_ref, rows_ref, tail_ref, z_ref, kin_ref, had_ref, sum_ref, row_sem, col_sem = refs[-9:]
+    out_ref, cols_ref, rows_ref, tail_ref, z_ref, kin_ref, had_ref, sum_ref, row_sem, col_sem = refs
     rows, variants = rows_ref.shape
     columns = z_ref.shape[0]
     blocks, each, _ = cols_ref.shape
@@ -87,8 +86,8 @@
     probes = cols_ref[:, :, variants:].reshape(columns, -1)
     for a in range(chromosomes):
         sum_ref[group_ref[a]] += jnp.dot(had_ref[a], probes, preferred_element_type=F32)
-    for k, out_ref in enumerate(out_refs):
-        out_ref[...] = sum_ref[lax.rem(me_ref[0] + k, groups)].astype(BF16)
+    for k in range(groups):
+        out_ref[k] = sum_ref[lax.rem(me_ref[0] + k, groups)].astype(BF16)
 
 
 def apply(me, own, other, cols, snp_counts, group_of, pair_mask, groups):
@@ -100,9 +99,9 @@
     vmem = pl.BlockSpec(memory_space=pltpu.VMEM)
     return pl.pallas_call(
         apply_kernel,
-        out_shape=[jax.ShapeDtypeStruct((rows, samples), BF16)] * groups,
+        out_shape=jax.ShapeDtypeStruct((groups, rows, samples), BF16),
         in_specs=[smem] * 4 + [pl.BlockSpec(memory_space=pl.ANY)] * 3,
-        out_specs=[vmem] * groups,
+        out_specs=vmem,
         scratch_shapes=[
             pltpu.VMEM(cols.shape, BF16),
             pltpu.VMEM((rows, variants), BF16),
@@ -155,14 +154,17 @@
     own = lax.all_gather(local, "c", axis=0, tiled=False)
     other = shifted(own, "v", 1)
     me = jnp.stack([c, v]).astype(jnp.int32)
-    parts = apply(me, own, other, cols, snp_counts, group_of, pair_mask, groups)
+    part = apply(me, own, other, cols, snp_counts, group_of, pair_mask, groups)
 
-    sums = parts[0].astype(F32)
-    for k in (2, 1, 3):
-        sums = sums + shifted(parts[k], "c", k).astype(F32)
-    total = sums.astype(BF16)
-    across = shifted(total, "v", 1)
-    return (total.astype(F32) + across.astype(F32)).astype(BF16)[None]
+    part = (part.astype(F32) + shifted(part, "v", 1).astype(F32)).astype(BF16)
+    pair = [(2 * i, 2 * ((i + 2) % groups)) for i in range(groups)]
+    pair += [(2 * i + 1, 2 * ((i + 1) % groups) + 1) for i in range(groups)]
+    last = [(2 * i + 1, 2 * ((i + 3) % groups) + 1) for i in range(groups)]
+    first = lax.ppermute(jnp.where(v == 0, part[2], part[1]), ("c", "v"), pair)
+    second = lax.ppermute(part[3], ("c", "v"), last)
+    mine = first.astype(F32) + jnp.where(v == 0, part[0], second).astype(F32)
+    mine = mine.astype(BF16)
+    return (mine.astype(F32) + shifted(mine, "v", 1).astype(F32)).astype(BF16)[None]
 
 
 def solution(mesh):

time: 83.4 us -> 82.5 us (0.989)
  waiting for transfers between devices: 10.8 us -> 9.48 us
    ppermute x0 -> x2, starting transfers between devices: none -> 5.54 us  [the longest x1 5.46 us: body(): second = lax.ppermute(part[3], ('c', 'v'), last)]
    ppermute x5 -> x3, starting transfers between devices: 17.4 us -> 12.1 us  [shifted(): return lax.ppermute(x, axis, [(i, (i + k) % n) for i in range(n)])]
    ppermute x5 -> x3, waiting for transfers between devices: 8.31 us -> 4.31 us  [shifted(): return lax.ppermute(x, axis, [(i, (i + k) % n) for i in range(n)])]
    ppermute x0 -> x2, waiting for transfers between devices: none -> 2.67 us  [the longest x1 1.72 us: body(): second = lax.ppermute(part[3], ('c', 'v'), last)]
  transfers between devices with their start and end apart: 6 -> 6, of which waited for: 5 -> 6; matrix products, arithmetic and copies ran while one was open for 0% -> 0% of each run, Pallas kernels for 0% -> 0%
where the time goes in v2:
time: 82.5 us; the launch traced here: 82.1 us
  blocking collectives  33.7 us (41%)
  starting transfers between devices  24.5 us (30%)
  Pallas kernels  9.86 us (12%)
  waiting for transfers between devices  9.48 us (11%)
  other arithmetic  2.72 us (3%)
  local copies, waits for them, and re-layouts  1.68 us (2%)
    all_to_all x1, blocking collectives, body(): mine = lax.all_to_all(codes, ('c', 'l'), 0, 0, tiled=True)  17 us
    all_gather x1, blocking collectives, body(): own = lax.all_gather(local, 'c', axis=0, tiled=False)  16.7 us
    ppermute x3, starting transfers between devices, shifted(): return lax.ppermute(x, axis, [(i, (i + k) % n) for i in range(n)])  12.1 us
    pallas_call x1, Pallas kernels, apply(): pl.pallas_call(apply_kernel, out_shape=jax.ShapeDtypeStruct((groups, rows...  9.86 us
    all_to_all x1, starting transfers between devices, body(): lax.all_to_all(jnp.broadcast_to(held[None], (plane, *held.shape)), ('y',...  6.9 us
    ppermute x1, starting transfers between devices, body(): second = lax.ppermute(part[3], ('c', 'v'), last)  5.46 us
    ppermute x3, waiting for transfers between devices, shifted(): return lax.ppermute(x, axis, [(i, (i + k) % n) for i in range(n)])  4.31 us
    all_to_all x1, waiting for transfers between devices, body(): lax.all_to_all(jnp.broadcast_to(held[None], (plane, *held.shape)), ('y',...  2.5 us
  transfers between devices with their start and end apart: 6, of which 6 were waited for; matrix products, arithmetic and copies ran while one was open for 0% of the time, Pallas kernels for 0%

profile of v2, /device:TPU:1, one launch (start us, length us, event | category | flops | bytes accessed | tf_op | source)
XLA Modules:
  0.0 82.1 jit_solution(16284749690041967402)
XLA Ops:
  0.0 0.9 %convert_element_type.39 = bf16[64,512]{1,0:T(8,128)(2,1)S(1)} convert(s32[64,512]{1,0:T(8,128)} %param.8) | non-fusion elementwise | flops 32768 | bytes 196608 | tf_op jit(solution)/shard_map/convert_element_type | solution.py:132
  0.9 0.7 pad_maximum_fusion
  1.7 17.0 %all_to_all.10 = bf16[8,16,640]{2,1,0:T(8,128)(2,1)S(1)} all-to-all(bf16[8,16,640]{2,1,0:T(8,128)(2,1)S(1)} %bitcast.26), channel_id=1, replica_groups=mesh['c'=4,'y'=4,'x'=4,'l'=2,'v'=2] {'c','l'}, dimensions={0} | all-to-all | bytes 327680 | tf_op jit(solution)/shard_map/all_to_all | solution.py:136
  18.7 1.5 %broadcast_in_dim.35 = bf16[16,32,2176]{2,1,0:T(8,128)(2,1)} broadcast(bf16[32,2176]{1,0:T(8,128)(2,1)S(1)} %bitcast.30), dimensions={1,2} | broadcast | bytes 2367488 | tf_op jit(solution)/shard_map/broadcast_in_dim | solution.py:143
  20.2 0.0 copy-start.4
  20.2 0.0 copy-start.3
  20.2 0.0 copy-start.1
  20.2 0.0 copy-start.2
  20.3 6.9 %all-to-all-start.1 = ((bf16[16,32,2176]{2,1,0:T(8,128)(2,1)}), bf16[16,32,2176]{2,1,0:T(8,128)(2,1)S(1)}, u32[]{:S(2)}, u32[]{:S(2)}) async-start(bf16[16,32,2176]{2,1,0:T(8,128)(2,1)} %broadcast_in_dim.35), calls=%async_computation.1 | async-start | bytes 4456448 | tf_op jit(solution)/shard_map/all_to_all | solution.py:142
  27.2 0.0 copy-done.4
  27.2 0.1 pad.5.clone
  27.3 0.0 copy-done.3
  27.3 0.1 maximum_maximum_fusion
  27.5 16.7 %all-gather = bf16[1600,256]{1,0:T(8,128)(2,1)S(1)} all-gather(bf16[400,256]{1,0:T(8,128)(2,1)S(1)} %maximum_maximum_fusion), channel_id=2, replica_groups=mesh['c'=4,'y'=4,'x'=4,'l'=2,'v'=2] {'c'}, dimensions={0}, use_global_device_ids=true | all-gather | bytes 1024000 | tf_op jit(solution)/shard_map/all_gather | solution.py:154
  44.2 5.1 %collective-permute-start = (bf16[4,400,256]{2,1,0:T(8,128)(2,1)S(1)}, bf16[4,400,256]{2,1,0:T(8,128)(2,1)}, u32[]{:S(2)}, u32[]{:S(2)}) collective-permute-start(bf16[4,400,256]{2,1,0:T(8,128)(2,1)S(1)} %bitcast.24), channel_id=1, source_target_pairs={{0,1},{1,0},{2,3},{3,2},{4,5},{5,4},{6,7},{7,6},{8,9},{9,8},{10,11... | collective-permute-start | bytes 2457608 | tf_op jit(solution)/shard_map/ppermute | solution.py:123
  49.3 0.1 pad_add_fusion.me_ref
  49.4 2.0 %collective-permute-done.other_hbm = bf16[4,400,256]{2,1,0:T(8,128)(2,1)} collective-permute-done((bf16[4,400,256]{2,1,0:T(8,128)(2,1)S(1)}, bf16[4,400,256]{2,1,0:T(8,128)(2,1)}, u32[]{:S(2)}, u32[]{:S(2)}) %collective-permute-start) | collective-permute-done | bytes 819232 | tf_op jit(solution)/shard_map/ppermute | solution.py:123
  51.4 2.5 %all-to-all-done.1.cols_hbm = bf16[16,32,2176]{2,1,0:T(8,128)(2,1)S(1)} async-done(((bf16[16,32,2176]{2,1,0:T(8,128)(2,1)}), bf16[16,32,2176]{2,1,0:T(8,128)(2,1)S(1)}, u32[]{:S(2)}, u32[]{:S(2)}) %all-to-all-start.1) | async-done | bytes 2228256 | tf_op jit(solution)/shard_map/all_to_all | solution.py:142
  53.9 0.0 copy-done
  53.9 0.0 copy-done.1
  53.9 0.0 copy-done.2
  53.9 9.9 %apply.1 = bf16[4,384,128]{2,1,0:T(8,128)(2,1)S(1)} custom-call(s32[2]{0:T(128)S(1)} %pad_add_fusion.me_ref, s32[8]{0:T(128)S(1)} %copy-done.1, s32[8]{0:T(128)S(1)} %copy-done.2, s32[8,8]{1,0:T(8,128)S(1)} %copy-done, bf16[4,400,256]{2,1,0:T(8,128)(2,1)S(1)} %bitcast.25, bf16[4,400,256]{2,1,0:T(8,128)(2,1)} %collective-permute-done.other_hbm, ...), custom_call_target="tpu_custom_call" | custom-call | tf_op jit(solution)/shard_map/apply/pallas_call | solution.py:100
  63.8 6.2 %collective-permute-start.1 = (bf16[4,384,128]{2,1,0:T(8,128)(2,1)S(1)}, bf16[4,384,128]{2,1,0:T(8,128)(2,1)S(1)}, u32[]{:S(2)}, u32[]{:S(2)}) collective-permute-start(bf16[4,384,128]{2,1,0:T(8,128)(2,1)S(1)} %apply.1), channel_id=1, source_target_pairs={{0,1},{1,0},{2,3},{3,2},{4,5},{5,4},{6,7},{7,6},{8,9},{9,8},{10,11... | collective-permute-start | bytes 1179656 | tf_op jit(solution)/shard_map/ppermute | solution.py:123
  69.9 1.3 %collective-permute-done.1 = bf16[4,384,128]{2,1,0:T(8,128)(2,1)S(1)} collective-permute-done((bf16[4,384,128]{2,1,0:T(8,128)(2,1)S(1)}, bf16[4,384,128]{2,1,0:T(8,128)(2,1)S(1)}, u32[]{:S(2)}, u32[]{:S(2)}) %collective-permute-start.1) | collective-permute-done | bytes 393248 | tf_op jit(solution)/shard_map/ppermute | solution.py:123
  71.3 0.1 add_convert_fusion
  71.4 0.1 collective-permute-start.2
  71.5 5.5 %collective-permute-start.3 = (bf16[384,128]{1,0:T(8,128)(2,1)S(1)}, bf16[384,128]{1,0:T(8,128)(2,1)S(1)}, u32[]{:S(2)}, u32[]{:S(2)}) collective-permute-start(bf16[384,128]{1,0:T(8,128)(2,1)S(1)} %get-tuple-element.5), channel_id=1, source_target_pairs={{1,193},{65,1},{129,65},{193,129},{3,195},{67,3},{131,67},{195,131... | collective-permute-start | bytes 294920 | tf_op jit(solution)/shard_map/ppermute | solution.py:164
  77.0 0.9 %collective-permute-done.2 = bf16[384,128]{1,0:T(8,128)(2,1)S(1)} collective-permute-done((bf16[384,128]{1,0:T(8,128)(2,1)S(1)}, bf16[384,128]{1,0:T(8,128)(2,1)S(1)}, u32[]{:S(2)}, u32[]{:S(2)}) %collective-permute-start.2) | collective-permute-done | bytes 98336 | tf_op jit(solution)/shard_map/ppermute | solution.py:163
  77.9 1.7 %collective-permute-done.3 = bf16[384,128]{1,0:T(8,128)(2,1)S(1)} collective-permute-done((bf16[384,128]{1,0:T(8,128)(2,1)S(1)}, bf16[384,128]{1,0:T(8,128)(2,1)S(1)}, u32[]{:S(2)}, u32[]{:S(2)}) %collective-permute-start.3) | collective-permute-done | bytes 98336 | tf_op jit(solution)/shard_map/ppermute | solution.py:164
  79.7 0.8 %collective-permute-start.4 = (bf16[384,128]{1,0:T(8,128)(2,1)S(1)}, bf16[384,128]{1,0:T(8,128)(2,1)S(1)}, u32[]{:S(2)}, u32[]{:S(2)}) collective-permute-start(bf16[384,128]{1,0:T(8,128)(2,1)S(1)} %add_convert_fusion.2), channel_id=1, source_target_pairs={{0,1},{1,0},{2,3},{3,2},{4,5},{5,4},{6,7},{7,6},{8,9},{9,8},{10,11... | collective-permute-start | bytes 294920 | tf_op jit(solution)/shard_map/ppermute | solution.py:123
  80.5 0.9 %collective-permute-done.4 = bf16[384,128]{1,0:T(8,128)(2,1)S(1)} collective-permute-done((bf16[384,128]{1,0:T(8,128)(2,1)S(1)}, bf16[384,128]{1,0:T(8,128)(2,1)S(1)}, u32[]{:S(2)}, u32[]{:S(2)}) %collective-permute-start.4) | collective-permute-done | bytes 98336 | tf_op jit(solution)/shard_map/ppermute | solution.py:123
  81.5 0.7 fusion
  (16 shorter events, 0.2 us)
Async XLA Ops:
  20.2 6.9 %copy-start.4 = (f32[256]{0:T(256)S(1)}, f32[256]{0:T(256)}, u32[]{:S(2)}) copy-start(f32[256]{0:T(256)} %param.9) | copy-start | bytes 3076
  20.2 7.1 %copy-start.3 = (s32[384,256]{1,0:T(8,128)S(1)}, s32[384,256]{1,0:T(8,128)}, u32[]{:S(2)}) copy-start(s32[384,256]{1,0:T(8,128)} %param.7) | copy-start | bytes 1179652
  20.2 33.6 %copy-start = (s32[8,8]{1,0:T(8,128)S(1)}, s32[8,8]{1,0:T(8,128)}, u32[]{:S(2)}) copy-start(s32[8,8]{1,0:T(8,128)} %mask_ref.1) | copy-start | bytes 772
  20.2 33.6 %copy-start.1 = (s32[8]{0:T(128)S(1)}, s32[8]{0:T(128)}, u32[]{:S(2)}) copy-start(s32[8]{0:T(128)} %counts_ref.1) | copy-start | bytes 100
  20.2 33.6 %copy-start.2 = (s32[8]{0:T(128)S(1)}, s32[8]{0:T(128)}, u32[]{:S(2)}) copy-start(s32[8]{0:T(128)} %group_ref.1) | copy-start | bytes 100
  20.3 33.6 %all-to-all-start.1 = ((bf16[16,32,2176]{2,1,0:T(8,128)(2,1)}), bf16[16,32,2176]{2,1,0:T(8,128)(2,1)S(1)}, u32[]{:S(2)}, u32[]{:S(2)}) async-start(bf16[16,32,2176]{2,1,0:T(8,128)(2,1)} %broadcast_in_dim.35), calls=%async_computation.1 | async-start | bytes 4456448 | tf_op jit(solution)/shard_map/all_to_all | solution.py:142
  44.2 7.2 %collective-permute-start = (bf16[4,400,256]{2,1,0:T(8,128)(2,1)S(1)}, bf16[4,400,256]{2,1,0:T(8,128)(2,1)}, u32[]{:S(2)}, u32[]{:S(2)}) collective-permute-start(bf16[4,400,256]{2,1,0:T(8,128)(2,1)S(1)} %bitcast.24), channel_id=1, source_target_pairs={{0,1},{1,0},{2,3},{3,2},{4,5},{5,4},{6,7},{7,6},{8,9},{9,8},{10,11... | collective-permute-start | bytes 2457608 | tf_op jit(solution)/shard_map/ppermute | solution.py:123
  63.8 7.5 %collective-permute-start.1 = (bf16[4,384,128]{2,1,0:T(8,128)(2,1)S(1)}, bf16[4,384,128]{2,1,0:T(8,128)(2,1)S(1)}, u32[]{:S(2)}, u32[]{:S(2)}) collective-permute-start(bf16[4,384,128]{2,1,0:T(8,128)(2,1)S(1)} %apply.1), channel_id=1, source_target_pairs={{0,1},{1,0},{2,3},{3,2},{4,5},{5,4},{6,7},{7,6},{8,9},{9,8},{10,11... | collective-permute-start | bytes 1179656 | tf_op jit(solution)/shard_map/ppermute | solution.py:123
  71.4 6.5 %collective-permute-start.2 = (bf16[384,128]{1,0:T(8,128)(2,1)S(1)}, bf16[384,128]{1,0:T(8,128)(2,1)S(1)}, u32[]{:S(2)}, u32[]{:S(2)}) collective-permute-start(bf16[384,128]{1,0:T(8,128)(2,1)S(1)} %get-tuple-element.6), channel_id=1, source_target_pairs={{0,128},{64,192},{128,0},{192,64},{1,65},{65,129},{129,193},{193,1... | collective-permute-start | bytes 294920 | tf_op jit(solution)/shard_map/ppermute | solution.py:163
  71.5 8.1 %collective-permute-start.3 = (bf16[384,128]{1,0:T(8,128)(2,1)S(1)}, bf16[384,128]{1,0:T(8,128)(2,1)S(1)}, u32[]{:S(2)}, u32[]{:S(2)}) collective-permute-start(bf16[384,128]{1,0:T(8,128)(2,1)S(1)} %get-tuple-element.5), channel_id=1, source_target_pairs={{1,193},{65,1},{129,65},{193,129},{3,195},{67,3},{131,67},{195,131... | collective-permute-start | bytes 294920 | tf_op jit(solution)/shard_map/ppermute | solution.py:164
  79.7 1.8 %collective-permute-start.4 = (bf16[384,128]{1,0:T(8,128)(2,1)S(1)}, bf16[384,128]{1,0:T(8,128)(2,1)S(1)}, u32[]{:S(2)}, u32[]{:S(2)}) collective-permute-start(bf16[384,128]{1,0:T(8,128)(2,1)S(1)} %add_convert_fusion.2), channel_id=1, source_target_pairs={{0,1},{1,0},{2,3},{3,2},{4,5},{5,4},{6,7},{7,6},{8,9},{9,8},{10,11... | collective-permute-start | bytes 294920 | tf_op jit(solution)/shard_map/ppermute | solution.py:123

commit v3 on v2

--- a/solution.py
+++ b/solution.py
@@ -25,7 +25,7 @@
 def apply_kernel(
     me_ref, counts_ref, group_ref, mask_ref, own_hbm, other_hbm, cols_hbm, *refs
 ):
-    out_ref, cols_ref, rows_ref, tail_ref, z_ref, kin_ref, had_ref, sum_ref, row_sem, col_sem = refs
+    keep_ref, send_ref, cols_ref, rows_ref, tail_ref, z_ref, kin_ref, had_ref, sum_ref, row_sem, col_sem = refs
     rows, variants = rows_ref.shape
     columns = z_ref.shape[0]
     blocks, each, _ = cols_ref.shape
@@ -60,12 +60,11 @@
         member = (lane >= first) & (lane < end)
         denominator = jnp.sum(jnp.where(member, spread, 0.0), axis=1, keepdims=True)
         here = start + lax.broadcasted_iota(jnp.int32, (1, WINDOW), 1)
-        own = jnp.where((here >= first) & (here < end), 1.0 / denominator, 0.0)
-        window = rows_ref[:, pl.ds(start, WINDOW)].astype(F32)
-        weighted = (window * own).astype(BF16)
+        member = ((here >= first) & (here < end)).astype(F32).astype(BF16)
+        window = rows_ref[:, pl.ds(start, WINDOW)] * member
         kin_ref[a] = lax.dot_general(
-            weighted, z_ref[:, pl.ds(start, WINDOW)], NT, preferred_element_type=F32
-        )
+            window, z_ref[:, pl.ds(start, WINDOW)], NT, preferred_element_type=F32
+        ) * (1.0 / denominator)
     pairs = [[mask_ref[a, b].astype(F32) for b in range(chromosomes)] for a in range(chromosomes)]
     high = 16
 
@@ -86,8 +85,9 @@
     probes = cols_ref[:, :, variants:].reshape(columns, -1)
     for a in range(chromosomes):
         sum_ref[group_ref[a]] += jnp.dot(had_ref[a], probes, preferred_element_type=F32)
-    for k in range(groups):
-        out_ref[k] = sum_ref[lax.rem(me_ref[0] + k, groups)].astype(BF16)
+    for out_ref, core in ((keep_ref, me_ref[1]), (send_ref, 1 - me_ref[1])):
+        for slot, k in enumerate((2 - core, 3 * core)):
+            out_ref[slot] = sum_ref[lax.rem(me_ref[0] + k, groups)].astype(BF16)
 
 
 def apply(me, own, other, cols, snp_counts, group_of, pair_mask, groups):
@@ -99,9 +99,9 @@
     vmem = pl.BlockSpec(memory_space=pltpu.VMEM)
     return pl.pallas_call(
         apply_kernel,
-        out_shape=jax.ShapeDtypeStruct((groups, rows, samples), BF16),
+        out_shape=[jax.ShapeDtypeStruct((groups // 2, rows, samples), BF16)] * 2,
         in_specs=[smem] * 4 + [pl.BlockSpec(memory_space=pl.ANY)] * 3,
-        out_specs=vmem,
+        out_specs=[vmem] * 2,
         scratch_shapes=[
             pltpu.VMEM(cols.shape, BF16),
             pltpu.VMEM((rows, variants), BF16),
@@ -154,15 +154,15 @@
     own = lax.all_gather(local, "c", axis=0, tiled=False)
     other = shifted(own, "v", 1)
     me = jnp.stack([c, v]).astype(jnp.int32)
-    part = apply(me, own, other, cols, snp_counts, group_of, pair_mask, groups)
+    keep, send = apply(me, own, other, cols, snp_counts, group_of, pair_mask, groups)
 
-    part = (part.astype(F32) + shifted(part, "v", 1).astype(F32)).astype(BF16)
+    chip = (keep.astype(F32) + shifted(send, "v", 1).astype(F32)).astype(BF16)
     pair = [(2 * i, 2 * ((i + 2) % groups)) for i in range(groups)]
     pair += [(2 * i + 1, 2 * ((i + 1) % groups) + 1) for i in range(groups)]
     last = [(2 * i + 1, 2 * ((i + 3) % groups) + 1) for i in range(groups)]
-    first = lax.ppermute(jnp.where(v == 0, part[2], part[1]), ("c", "v"), pair)
-    second = lax.ppermute(part[3], ("c", "v"), last)
-    mine = first.astype(F32) + jnp.where(v == 0, part[0], second).astype(F32)
+    first = lax.ppermute(chip[0], ("c", "v"), pair)
+    second = lax.ppermute(chip[1], ("c", "v"), last)
+    mine = first.astype(F32) + jnp.where(v == 0, chip[1], second).astype(F32)
     mine = mine.astype(BF16)
     return (mine.astype(F32) + shifted(mine, "v", 1).astype(F32)).astype(BF16)[None]
 

time: 82.5 us -> 82.1 us (level)
  no operation moved by 1% of the time
where the time goes in v3:
time: 82.1 us; the launch traced here: 81.7 us
  blocking collectives  33.7 us (41%)
  starting transfers between devices  24.6 us (30%)
  Pallas kernels  9.72 us (12%)
  waiting for transfers between devices  9.19 us (11%)
  other arithmetic  2.65 us (3%)
  local copies, waits for them, and re-layouts  1.7 us (2%)
    all_to_all x1, blocking collectives, body(): mine = lax.all_to_all(codes, ('c', 'l'), 0, 0, tiled=True)  17 us
    all_gather x1, blocking collectives, body(): own = lax.all_gather(local, 'c', axis=0, tiled=False)  16.7 us
    ppermute x3, starting transfers between devices, shifted(): return lax.ppermute(x, axis, [(i, (i + k) % n) for i in range(n)])  12.1 us
    pallas_call x1, Pallas kernels, apply(): pl.pallas_call(apply_kernel, out_shape=[jax.ShapeDtypeStruct((groups // 2...  9.72 us
    all_to_all x1, starting transfers between devices, body(): lax.all_to_all(jnp.broadcast_to(held[None], (plane, *held.shape)), ('y',...  6.9 us
    ppermute x1, starting transfers between devices, body(): second = lax.ppermute(chip[1], ('c', 'v'), last)  5.46 us
    ppermute x3, waiting for transfers between devices, shifted(): return lax.ppermute(x, axis, [(i, (i + k) % n) for i in range(n)])  4.03 us
    all_to_all x1, waiting for transfers between devices, body(): lax.all_to_all(jnp.broadcast_to(held[None], (plane, *held.shape)), ('y',...  2.5 us
  transfers between devices with their start and end apart: 6, of which 6 were waited for; matrix products, arithmetic and copies ran while one was open for 0% of the time, Pallas kernels for 0%

profile of v3, /device:TPU:1, one launch (start us, length us, event | category | flops | bytes accessed | tf_op | source)
XLA Modules:
  0.0 81.7 jit_solution(16855734225498054337)
XLA Ops:
  0.0 0.9 %convert_element_type.39 = bf16[64,512]{1,0:T(8,128)(2,1)S(1)} convert(s32[64,512]{1,0:T(8,128)} %param.8) | non-fusion elementwise | flops 32768 | bytes 196608 | tf_op jit(solution)/shard_map/convert_element_type | solution.py:132
  0.9 0.7 pad_maximum_fusion
  1.7 17.0 %all_to_all.10 = bf16[8,16,640]{2,1,0:T(8,128)(2,1)S(1)} all-to-all(bf16[8,16,640]{2,1,0:T(8,128)(2,1)S(1)} %bitcast.22), channel_id=1, replica_groups=mesh['c'=4,'y'=4,'x'=4,'l'=2,'v'=2] {'c','l'}, dimensions={0} | all-to-all | bytes 327680 | tf_op jit(solution)/shard_map/all_to_all | solution.py:136
  18.7 1.5 %broadcast_in_dim.35 = bf16[16,32,2176]{2,1,0:T(8,128)(2,1)} broadcast(bf16[32,2176]{1,0:T(8,128)(2,1)S(1)} %bitcast.26), dimensions={1,2} | broadcast | bytes 2367488 | tf_op jit(solution)/shard_map/broadcast_in_dim | solution.py:143
  20.2 0.0 copy-start.4
  20.2 0.0 copy-start
  20.2 0.0 copy-start.1
  20.2 0.0 copy-start.2
  20.3 6.9 %all-to-all-start.1 = ((bf16[16,32,2176]{2,1,0:T(8,128)(2,1)}), bf16[16,32,2176]{2,1,0:T(8,128)(2,1)S(1)}, u32[]{:S(2)}, u32[]{:S(2)}) async-start(bf16[16,32,2176]{2,1,0:T(8,128)(2,1)} %broadcast_in_dim.35), calls=%async_computation.1 | async-start | bytes 4456448 | tf_op jit(solution)/shard_map/all_to_all | solution.py:142
  27.2 0.0 copy-done.4
  27.2 0.1 pad.5.clone
  27.3 0.0 copy-done.3
  27.3 0.1 maximum_maximum_fusion
  27.5 16.7 %all-gather = bf16[1600,256]{1,0:T(8,128)(2,1)S(1)} all-gather(bf16[400,256]{1,0:T(8,128)(2,1)S(1)} %maximum_maximum_fusion), channel_id=2, replica_groups=mesh['c'=4,'y'=4,'x'=4,'l'=2,'v'=2] {'c'}, dimensions={0}, use_global_device_ids=true | all-gather | bytes 1024000 | tf_op jit(solution)/shard_map/all_gather | solution.py:154
  44.2 5.1 %collective-permute-start = (bf16[4,400,256]{2,1,0:T(8,128)(2,1)S(1)}, bf16[4,400,256]{2,1,0:T(8,128)(2,1)}, u32[]{:S(2)}, u32[]{:S(2)}) collective-permute-start(bf16[4,400,256]{2,1,0:T(8,128)(2,1)S(1)} %bitcast.20), channel_id=1, source_target_pairs={{0,1},{1,0},{2,3},{3,2},{4,5},{5,4},{6,7},{7,6},{8,9},{9,8},{10,11... | collective-permute-start | bytes 2457608 | tf_op jit(solution)/shard_map/ppermute | solution.py:123
  49.3 0.1 pad_add_fusion.me_ref
  49.4 2.0 %collective-permute-done.other_hbm = bf16[4,400,256]{2,1,0:T(8,128)(2,1)} collective-permute-done((bf16[4,400,256]{2,1,0:T(8,128)(2,1)S(1)}, bf16[4,400,256]{2,1,0:T(8,128)(2,1)}, u32[]{:S(2)}, u32[]{:S(2)}) %collective-permute-start) | collective-permute-done | bytes 819232 | tf_op jit(solution)/shard_map/ppermute | solution.py:123
  51.4 2.5 %all-to-all-done.1.cols_hbm = bf16[16,32,2176]{2,1,0:T(8,128)(2,1)S(1)} async-done(((bf16[16,32,2176]{2,1,0:T(8,128)(2,1)}), bf16[16,32,2176]{2,1,0:T(8,128)(2,1)S(1)}, u32[]{:S(2)}, u32[]{:S(2)}) %all-to-all-start.1) | async-done | bytes 2228256 | tf_op jit(solution)/shard_map/all_to_all | solution.py:142
  53.9 0.0 copy-done
  53.9 0.0 copy-done.1
  53.9 0.0 copy-done.2
  53.9 9.7 %apply.1 = (bf16[2,384,128]{2,1,0:T(8,128)(2,1)S(1)}, bf16[2,384,128]{2,1,0:T(8,128)(2,1)S(1)}) custom-call(s32[2]{0:T(128)S(1)} %pad_add_fusion.me_ref, s32[8]{0:T(128)S(1)} %copy-done.1, s32[8]{0:T(128)S(1)} %copy-done.2, s32[8,8]{1,0:T(8,128)S(1)} %copy-done, bf16[4,400,256]{2,1,0:T(8,128)(2,1)S(1)} %bitcast.21, ...), custom_call_target="tpu_custom_call" | custom-call | tf_op jit(solution)/shard_map/apply/pallas_call | solution.py:100
  63.6 6.2 %collective-permute-start.1 = (bf16[2,384,128]{2,1,0:T(8,128)(2,1)S(1)}, bf16[2,384,128]{2,1,0:T(8,128)(2,1)S(1)}, u32[]{:S(2)}, u32[]{:S(2)}) collective-permute-start(bf16[2,384,128]{2,1,0:T(8,128)(2,1)S(1)} %get-tuple-element.8), channel_id=1, source_target_pairs={{0,1},{1,0},{2,3},{3,2},{4,5},{5,4},{6,7},{7,6},{8,9},{9,8},{10,11... | collective-permute-start | bytes 589832 | tf_op jit(solution)/shard_map/ppermute | solution.py:123
  69.8 1.1 %collective-permute-done.1 = bf16[2,384,128]{2,1,0:T(8,128)(2,1)S(1)} collective-permute-done((bf16[2,384,128]{2,1,0:T(8,128)(2,1)S(1)}, bf16[2,384,128]{2,1,0:T(8,128)(2,1)S(1)}, u32[]{:S(2)}, u32[]{:S(2)}) %collective-permute-start.1) | collective-permute-done | bytes 196640 | tf_op jit(solution)/shard_map/ppermute | solution.py:123
  70.9 0.1 add_convert_fusion
  71.0 0.1 collective-permute-start.2
  71.0 5.5 %collective-permute-start.3 = (bf16[384,128]{1,0:T(8,128)(2,1)S(1)}, bf16[384,128]{1,0:T(8,128)(2,1)S(1)}, u32[]{:S(2)}, u32[]{:S(2)}) collective-permute-start(bf16[384,128]{1,0:T(8,128)(2,1)S(1)} %get-tuple-element.9), channel_id=1, source_target_pairs={{1,193},{65,1},{129,65},{193,129},{3,195},{67,3},{131,67},{195,131... | collective-permute-start | bytes 294920 | tf_op jit(solution)/shard_map/ppermute | solution.py:164
  76.5 0.9 %collective-permute-done.2 = bf16[384,128]{1,0:T(8,128)(2,1)S(1)} collective-permute-done((bf16[384,128]{1,0:T(8,128)(2,1)S(1)}, bf16[384,128]{1,0:T(8,128)(2,1)S(1)}, u32[]{:S(2)}, u32[]{:S(2)}) %collective-permute-start.2) | collective-permute-done | bytes 98336 | tf_op jit(solution)/shard_map/ppermute | solution.py:163
  77.5 1.7 %collective-permute-done.3 = bf16[384,128]{1,0:T(8,128)(2,1)S(1)} collective-permute-done((bf16[384,128]{1,0:T(8,128)(2,1)S(1)}, bf16[384,128]{1,0:T(8,128)(2,1)S(1)}, u32[]{:S(2)}, u32[]{:S(2)}) %collective-permute-start.3) | collective-permute-done | bytes 98336 | tf_op jit(solution)/shard_map/ppermute | solution.py:164
  79.2 0.8 %collective-permute-start.4 = (bf16[384,128]{1,0:T(8,128)(2,1)S(1)}, bf16[384,128]{1,0:T(8,128)(2,1)S(1)}, u32[]{:S(2)}, u32[]{:S(2)}) collective-permute-start(bf16[384,128]{1,0:T(8,128)(2,1)S(1)} %add_convert_fusion.2), channel_id=1, source_target_pairs={{0,1},{1,0},{2,3},{3,2},{4,5},{5,4},{6,7},{7,6},{8,9},{9,8},{10,11... | collective-permute-start | bytes 294920 | tf_op jit(solution)/shard_map/ppermute | solution.py:123
  80.1 0.9 %collective-permute-done.4 = bf16[384,128]{1,0:T(8,128)(2,1)S(1)} collective-permute-done((bf16[384,128]{1,0:T(8,128)(2,1)S(1)}, bf16[384,128]{1,0:T(8,128)(2,1)S(1)}, u32[]{:S(2)}, u32[]{:S(2)}) %collective-permute-start.4) | collective-permute-done | bytes 98336 | tf_op jit(solution)/shard_map/ppermute | solution.py:123
  81.0 0.7 fusion
  (16 shorter events, 0.2 us)
Async XLA Ops:
  20.2 6.9 %copy-start.4 = (f32[256]{0:T(256)S(1)}, f32[256]{0:T(256)}, u32[]{:S(2)}) copy-start(f32[256]{0:T(256)} %param.9) | copy-start | bytes 3076
  20.2 7.1 %copy-start.3 = (s32[384,256]{1,0:T(8,128)S(1)}, s32[384,256]{1,0:T(8,128)}, u32[]{:S(2)}) copy-start(s32[384,256]{1,0:T(8,128)} %param.7) | copy-start | bytes 1179652
  20.2 33.6 %copy-start = (s32[8,8]{1,0:T(8,128)S(1)}, s32[8,8]{1,0:T(8,128)}, u32[]{:S(2)}) copy-start(s32[8,8]{1,0:T(8,128)} %mask_ref.1) | copy-start | bytes 772
  20.2 33.6 %copy-start.1 = (s32[8]{0:T(128)S(1)}, s32[8]{0:T(128)}, u32[]{:S(2)}) copy-start(s32[8]{0:T(128)} %counts_ref.1) | copy-start | bytes 100
  20.2 33.6 %copy-start.2 = (s32[8]{0:T(128)S(1)}, s32[8]{0:T(128)}, u32[]{:S(2)}) copy-start(s32[8]{0:T(128)} %group_ref.1) | copy-start | bytes 100
  20.3 33.6 %all-to-all-start.1 = ((bf16[16,32,2176]{2,1,0:T(8,128)(2,1)}), bf16[16,32,2176]{2,1,0:T(8,128)(2,1)S(1)}, u32[]{:S(2)}, u32[]{:S(2)}) async-start(bf16[16,32,2176]{2,1,0:T(8,128)(2,1)} %broadcast_in_dim.35), calls=%async_computation.1 | async-start | bytes 4456448 | tf_op jit(solution)/shard_map/all_to_all | solution.py:142
  44.2 7.2 %collective-permute-start = (bf16[4,400,256]{2,1,0:T(8,128)(2,1)S(1)}, bf16[4,400,256]{2,1,0:T(8,128)(2,1)}, u32[]{:S(2)}, u32[]{:S(2)}) collective-permute-start(bf16[4,400,256]{2,1,0:T(8,128)(2,1)S(1)} %bitcast.20), channel_id=1, source_target_pairs={{0,1},{1,0},{2,3},{3,2},{4,5},{5,4},{6,7},{7,6},{8,9},{9,8},{10,11... | collective-permute-start | bytes 2457608 | tf_op jit(solution)/shard_map/ppermute | solution.py:123
  63.6 7.3 %collective-permute-start.1 = (bf16[2,384,128]{2,1,0:T(8,128)(2,1)S(1)}, bf16[2,384,128]{2,1,0:T(8,128)(2,1)S(1)}, u32[]{:S(2)}, u32[]{:S(2)}) collective-permute-start(bf16[2,384,128]{2,1,0:T(8,128)(2,1)S(1)} %get-tuple-element.8), channel_id=1, source_target_pairs={{0,1},{1,0},{2,3},{3,2},{4,5},{5,4},{6,7},{7,6},{8,9},{9,8},{10,11... | collective-permute-start | bytes 589832 | tf_op jit(solution)/shard_map/ppermute | solution.py:123
  71.0 6.5 %collective-permute-start.2 = (bf16[384,128]{1,0:T(8,128)(2,1)S(1)}, bf16[384,128]{1,0:T(8,128)(2,1)S(1)}, u32[]{:S(2)}, u32[]{:S(2)}) collective-permute-start(bf16[384,128]{1,0:T(8,128)(2,1)S(1)} %get-tuple-element.10), channel_id=1, source_target_pairs={{0,128},{64,192},{128,0},{192,64},{1,65},{65,129},{129,193},{193,1... | collective-permute-start | bytes 294920 | tf_op jit(solution)/shard_map/ppermute | solution.py:163
  71.0 8.1 %collective-permute-start.3 = (bf16[384,128]{1,0:T(8,128)(2,1)S(1)}, bf16[384,128]{1,0:T(8,128)(2,1)S(1)}, u32[]{:S(2)}, u32[]{:S(2)}) collective-permute-start(bf16[384,128]{1,0:T(8,128)(2,1)S(1)} %get-tuple-element.9), channel_id=1, source_target_pairs={{1,193},{65,1},{129,65},{193,129},{3,195},{67,3},{131,67},{195,131... | collective-permute-start | bytes 294920 | tf_op jit(solution)/shard_map/ppermute | solution.py:164
  79.2 1.8 %collective-permute-start.4 = (bf16[384,128]{1,0:T(8,128)(2,1)S(1)}, bf16[384,128]{1,0:T(8,128)(2,1)S(1)}, u32[]{:S(2)}, u32[]{:S(2)}) collective-permute-start(bf16[384,128]{1,0:T(8,128)(2,1)S(1)} %add_convert_fusion.2), channel_id=1, source_target_pairs={{0,1},{1,0},{2,3},{3,2},{4,5},{5,4},{6,7},{7,6},{8,9},{9,8},{10,11... | collective-permute-start | bytes 294920 | tf_op jit(solution)/shard_map/ppermute | solution.py:123

commit v4 on v3

--- a/solution.py
+++ b/solution.py
@@ -100,7 +100,7 @@
     return pl.pallas_call(
         apply_kernel,
         out_shape=[jax.ShapeDtypeStruct((groups // 2, rows, samples), BF16)] * 2,
-        in_specs=[smem] * 4 + [pl.BlockSpec(memory_space=pl.ANY)] * 3,
+        in_specs=[smem] * 4 + [vmem] * 2 + [pl.BlockSpec(memory_space=pl.ANY)],
         out_specs=[vmem] * 2,
         scratch_shapes=[
             pltpu.VMEM(cols.shape, BF16),

time: 82.1 us -> 81.7 us (level)
  no operation moved by 1% of the time
where the time goes in v4:
time: 81.7 us; the launch traced here: 81.4 us
  blocking collectives  33.7 us (41%)
  starting transfers between devices  24.5 us (30%)
  Pallas kernels  9.43 us (12%)
  waiting for transfers between devices  9.2 us (11%)
  other arithmetic  2.65 us (3%)
  local copies, waits for them, and re-layouts  1.7 us (2%)
    all_to_all x1, blocking collectives, body(): mine = lax.all_to_all(codes, ('c', 'l'), 0, 0, tiled=True)  17 us
    all_gather x1, blocking collectives, body(): own = lax.all_gather(local, 'c', axis=0, tiled=False)  16.7 us
    ppermute x3, starting transfers between devices, shifted(): return lax.ppermute(x, axis, [(i, (i + k) % n) for i in range(n)])  12.1 us
    pallas_call x1, Pallas kernels, apply(): pl.pallas_call(apply_kernel, out_shape=[jax.ShapeDtypeStruct((groups // 2...  9.43 us
    all_to_all x1, starting transfers between devices, body(): lax.all_to_all(jnp.broadcast_to(held[None], (plane, *held.shape)), ('y',...  6.9 us
    ppermute x1, starting transfers between devices, body(): second = lax.ppermute(chip[1], ('c', 'v'), last)  5.46 us
    ppermute x3, waiting for transfers between devices, shifted(): return lax.ppermute(x, axis, [(i, (i + k) % n) for i in range(n)])  4.03 us
    all_to_all x1, waiting for transfers between devices, body(): lax.all_to_all(jnp.broadcast_to(held[None], (plane, *held.shape)), ('y',...  2.5 us
  transfers between devices with their start and end apart: 6, of which 6 were waited for; matrix products, arithmetic and copies ran while one was open for 0% of the time, Pallas kernels for 0%

profile of v4, /device:TPU:1, one launch (start us, length us, event | category | flops | bytes accessed | tf_op | source)
XLA Modules:
  0.0 81.4 jit_solution(11805218931505451712)
XLA Ops:
  0.0 0.9 %convert_element_type.39 = bf16[64,512]{1,0:T(8,128)(2,1)S(1)} convert(s32[64,512]{1,0:T(8,128)} %param.8) | non-fusion elementwise | flops 32768 | bytes 196608 | tf_op jit(solution)/shard_map/convert_element_type | solution.py:132
  0.9 0.7 pad_maximum_fusion
  1.7 17.0 %all_to_all.10 = bf16[8,16,640]{2,1,0:T(8,128)(2,1)S(1)} all-to-all(bf16[8,16,640]{2,1,0:T(8,128)(2,1)S(1)} %bitcast.22), channel_id=1, replica_groups=mesh['c'=4,'y'=4,'x'=4,'l'=2,'v'=2] {'c','l'}, dimensions={0} | all-to-all | bytes 327680 | tf_op jit(solution)/shard_map/all_to_all | solution.py:136
  18.7 1.5 %broadcast_in_dim.35 = bf16[16,32,2176]{2,1,0:T(8,128)(2,1)} broadcast(bf16[32,2176]{1,0:T(8,128)(2,1)S(1)} %bitcast.26), dimensions={1,2} | broadcast | bytes 2367488 | tf_op jit(solution)/shard_map/broadcast_in_dim | solution.py:143
  20.2 0.0 copy-start.4
  20.2 0.0 copy-start.3
  20.2 0.0 copy-start
  20.2 0.0 copy-start.2
  20.3 6.9 %all-to-all-start.1 = ((bf16[16,32,2176]{2,1,0:T(8,128)(2,1)}), bf16[16,32,2176]{2,1,0:T(8,128)(2,1)S(1)}, u32[]{:S(2)}, u32[]{:S(2)}) async-start(bf16[16,32,2176]{2,1,0:T(8,128)(2,1)} %broadcast_in_dim.35), calls=%async_computation.1 | async-start | bytes 4456448 | tf_op jit(solution)/shard_map/all_to_all | solution.py:142
  27.2 0.0 copy-done.4
  27.2 0.1 pad.5.clone
  27.3 0.0 copy-done.3
  27.3 0.1 maximum_maximum_fusion
  27.5 16.7 %all-gather = bf16[1600,256]{1,0:T(8,128)(2,1)S(1)} all-gather(bf16[400,256]{1,0:T(8,128)(2,1)S(1)} %maximum_maximum_fusion), channel_id=2, replica_groups=mesh['c'=4,'y'=4,'x'=4,'l'=2,'v'=2] {'c'}, dimensions={0}, use_global_device_ids=true | all-gather | bytes 1024000 | tf_op jit(solution)/shard_map/all_gather | solution.py:154
  44.2 5.1 %collective-permute-start = (bf16[4,400,256]{2,1,0:T(8,128)(2,1)S(1)}, bf16[4,400,256]{2,1,0:T(8,128)(2,1)}, u32[]{:S(2)}, u32[]{:S(2)}) collective-permute-start(bf16[4,400,256]{2,1,0:T(8,128)(2,1)S(1)} %bitcast.20), channel_id=1, source_target_pairs={{0,1},{1,0},{2,3},{3,2},{4,5},{5,4},{6,7},{7,6},{8,9},{9,8},{10,11... | collective-permute-start | bytes 2457608 | tf_op jit(solution)/shard_map/ppermute | solution.py:123
  49.3 0.1 pad_add_fusion.me_ref
  49.4 2.0 %collective-permute-done.other_hbm = bf16[4,400,256]{2,1,0:T(8,128)(2,1)} collective-permute-done((bf16[4,400,256]{2,1,0:T(8,128)(2,1)S(1)}, bf16[4,400,256]{2,1,0:T(8,128)(2,1)}, u32[]{:S(2)}, u32[]{:S(2)}) %collective-permute-start) | collective-permute-done | bytes 819232 | tf_op jit(solution)/shard_map/ppermute | solution.py:123
  51.4 2.5 %all-to-all-done.1.cols_hbm = bf16[16,32,2176]{2,1,0:T(8,128)(2,1)S(1)} async-done(((bf16[16,32,2176]{2,1,0:T(8,128)(2,1)}), bf16[16,32,2176]{2,1,0:T(8,128)(2,1)S(1)}, u32[]{:S(2)}, u32[]{:S(2)}) %all-to-all-start.1) | async-done | bytes 2228256 | tf_op jit(solution)/shard_map/all_to_all | solution.py:142
  53.9 0.0 copy-done
  53.9 0.0 copy-done.1
  53.9 0.0 copy-done.2
  53.9 9.4 %apply.1 = (bf16[2,384,128]{2,1,0:T(8,128)(2,1)S(1)}, bf16[2,384,128]{2,1,0:T(8,128)(2,1)S(1)}) custom-call(s32[2]{0:T(128)S(1)} %pad_add_fusion.me_ref, s32[8]{0:T(128)S(1)} %copy-done.1, s32[8]{0:T(128)S(1)} %copy-done.2, s32[8,8]{1,0:T(8,128)S(1)} %copy-done, bf16[4,400,256]{2,1,0:T(8,128)(2,1)S(1)} %bitcast.21, ...), custom_call_target="tpu_custom_call" | custom-call | tf_op jit(solution)/shard_map/apply/pallas_call | solution.py:100
  63.3 6.2 %collective-permute-start.1 = (bf16[2,384,128]{2,1,0:T(8,128)(2,1)S(1)}, bf16[2,384,128]{2,1,0:T(8,128)(2,1)S(1)}, u32[]{:S(2)}, u32[]{:S(2)}) collective-permute-start(bf16[2,384,128]{2,1,0:T(8,128)(2,1)S(1)} %get-tuple-element.8), channel_id=1, source_target_pairs={{0,1},{1,0},{2,3},{3,2},{4,5},{5,4},{6,7},{7,6},{8,9},{9,8},{10,11... | collective-permute-start | bytes 589832 | tf_op jit(solution)/shard_map/ppermute | solution.py:123
  69.5 1.1 %collective-permute-done.1 = bf16[2,384,128]{2,1,0:T(8,128)(2,1)S(1)} collective-permute-done((bf16[2,384,128]{2,1,0:T(8,128)(2,1)S(1)}, bf16[2,384,128]{2,1,0:T(8,128)(2,1)S(1)}, u32[]{:S(2)}, u32[]{:S(2)}) %collective-permute-start.1) | collective-permute-done | bytes 196640 | tf_op jit(solution)/shard_map/ppermute | solution.py:123
  70.6 0.1 add_convert_fusion
  70.7 0.1 collective-permute-start.2
  70.7 5.5 %collective-permute-start.3 = (bf16[384,128]{1,0:T(8,128)(2,1)S(1)}, bf16[384,128]{1,0:T(8,128)(2,1)S(1)}, u32[]{:S(2)}, u32[]{:S(2)}) collective-permute-start(bf16[384,128]{1,0:T(8,128)(2,1)S(1)} %get-tuple-element.9), channel_id=1, source_target_pairs={{1,193},{65,1},{129,65},{193,129},{3,195},{67,3},{131,67},{195,131... | collective-permute-start | bytes 294920 | tf_op jit(solution)/shard_map/ppermute | solution.py:164
  76.2 0.9 %collective-permute-done.2 = bf16[384,128]{1,0:T(8,128)(2,1)S(1)} collective-permute-done((bf16[384,128]{1,0:T(8,128)(2,1)S(1)}, bf16[384,128]{1,0:T(8,128)(2,1)S(1)}, u32[]{:S(2)}, u32[]{:S(2)}) %collective-permute-start.2) | collective-permute-done | bytes 98336 | tf_op jit(solution)/shard_map/ppermute | solution.py:163
  77.2 1.7 %collective-permute-done.3 = bf16[384,128]{1,0:T(8,128)(2,1)S(1)} collective-permute-done((bf16[384,128]{1,0:T(8,128)(2,1)S(1)}, bf16[384,128]{1,0:T(8,128)(2,1)S(1)}, u32[]{:S(2)}, u32[]{:S(2)}) %collective-permute-start.3) | collective-permute-done | bytes 98336 | tf_op jit(solution)/shard_map/ppermute | solution.py:164
  78.9 0.8 %collective-permute-start.4 = (bf16[384,128]{1,0:T(8,128)(2,1)S(1)}, bf16[384,128]{1,0:T(8,128)(2,1)S(1)}, u32[]{:S(2)}, u32[]{:S(2)}) collective-permute-start(bf16[384,128]{1,0:T(8,128)(2,1)S(1)} %add_convert_fusion.2), channel_id=1, source_target_pairs={{0,1},{1,0},{2,3},{3,2},{4,5},{5,4},{6,7},{7,6},{8,9},{9,8},{10,11... | collective-permute-start | bytes 294920 | tf_op jit(solution)/shard_map/ppermute | solution.py:123
  79.8 0.9 %collective-permute-done.4 = bf16[384,128]{1,0:T(8,128)(2,1)S(1)} collective-permute-done((bf16[384,128]{1,0:T(8,128)(2,1)S(1)}, bf16[384,128]{1,0:T(8,128)(2,1)S(1)}, u32[]{:S(2)}, u32[]{:S(2)}) %collective-permute-start.4) | collective-permute-done | bytes 98336 | tf_op jit(solution)/shard_map/ppermute | solution.py:123
  80.7 0.7 fusion
  (16 shorter events, 0.2 us)
Async XLA Ops:
  20.2 6.9 %copy-start.4 = (f32[256]{0:T(256)S(1)}, f32[256]{0:T(256)}, u32[]{:S(2)}) copy-start(f32[256]{0:T(256)} %param.9) | copy-start | bytes 3076
  20.2 7.1 %copy-start.3 = (s32[384,256]{1,0:T(8,128)S(1)}, s32[384,256]{1,0:T(8,128)}, u32[]{:S(2)}) copy-start(s32[384,256]{1,0:T(8,128)} %param.7) | copy-start | bytes 1179652
  20.2 33.6 %copy-start = (s32[8,8]{1,0:T(8,128)S(1)}, s32[8,8]{1,0:T(8,128)}, u32[]{:S(2)}) copy-start(s32[8,8]{1,0:T(8,128)} %mask_ref.1) | copy-start | bytes 772
  20.2 33.6 %copy-start.1 = (s32[8]{0:T(128)S(1)}, s32[8]{0:T(128)}, u32[]{:S(2)}) copy-start(s32[8]{0:T(128)} %counts_ref.1) | copy-start | bytes 100
  20.2 33.6 %copy-start.2 = (s32[8]{0:T(128)S(1)}, s32[8]{0:T(128)}, u32[]{:S(2)}) copy-start(s32[8]{0:T(128)} %group_ref.1) | copy-start | bytes 100
  20.3 33.6 %all-to-all-start.1 = ((bf16[16,32,2176]{2,1,0:T(8,128)(2,1)}), bf16[16,32,2176]{2,1,0:T(8,128)(2,1)S(1)}, u32[]{:S(2)}, u32[]{:S(2)}) async-start(bf16[16,32,2176]{2,1,0:T(8,128)(2,1)} %broadcast_in_dim.35), calls=%async_computation.1 | async-start | bytes 4456448 | tf_op jit(solution)/shard_map/all_to_all | solution.py:142
  44.2 7.2 %collective-permute-start = (bf16[4,400,256]{2,1,0:T(8,128)(2,1)S(1)}, bf16[4,400,256]{2,1,0:T(8,128)(2,1)}, u32[]{:S(2)}, u32[]{:S(2)}) collective-permute-start(bf16[4,400,256]{2,1,0:T(8,128)(2,1)S(1)} %bitcast.20), channel_id=1, source_target_pairs={{0,1},{1,0},{2,3},{3,2},{4,5},{5,4},{6,7},{7,6},{8,9},{9,8},{10,11... | collective-permute-start | bytes 2457608 | tf_op jit(solution)/shard_map/ppermute | solution.py:123
  63.3 7.2 %collective-permute-start.1 = (bf16[2,384,128]{2,1,0:T(8,128)(2,1)S(1)}, bf16[2,384,128]{2,1,0:T(8,128)(2,1)S(1)}, u32[]{:S(2)}, u32[]{:S(2)}) collective-permute-start(bf16[2,384,128]{2,1,0:T(8,128)(2,1)S(1)} %get-tuple-element.8), channel_id=1, source_target_pairs={{0,1},{1,0},{2,3},{3,2},{4,5},{5,4},{6,7},{7,6},{8,9},{9,8},{10,11... | collective-permute-start | bytes 589832 | tf_op jit(solution)/shard_map/ppermute | solution.py:123
  70.7 6.5 %collective-permute-start.2 = (bf16[384,128]{1,0:T(8,128)(2,1)S(1)}, bf16[384,128]{1,0:T(8,128)(2,1)S(1)}, u32[]{:S(2)}, u32[]{:S(2)}) collective-permute-start(bf16[384,128]{1,0:T(8,128)(2,1)S(1)} %get-tuple-element.10), channel_id=1, source_target_pairs={{0,128},{64,192},{128,0},{192,64},{1,65},{65,129},{129,193},{193,1... | collective-permute-start | bytes 294920 | tf_op jit(solution)/shard_map/ppermute | solution.py:163
  70.7 8.1 %collective-permute-start.3 = (bf16[384,128]{1,0:T(8,128)(2,1)S(1)}, bf16[384,128]{1,0:T(8,128)(2,1)S(1)}, u32[]{:S(2)}, u32[]{:S(2)}) collective-permute-start(bf16[384,128]{1,0:T(8,128)(2,1)S(1)} %get-tuple-element.9), channel_id=1, source_target_pairs={{1,193},{65,1},{129,65},{193,129},{3,195},{67,3},{131,67},{195,131... | collective-permute-start | bytes 294920 | tf_op jit(solution)/shard_map/ppermute | solution.py:164
  78.9 1.8 %collective-permute-start.4 = (bf16[384,128]{1,0:T(8,128)(2,1)S(1)}, bf16[384,128]{1,0:T(8,128)(2,1)S(1)}, u32[]{:S(2)}, u32[]{:S(2)}) collective-permute-start(bf16[384,128]{1,0:T(8,128)(2,1)S(1)} %add_convert_fusion.2), channel_id=1, source_target_pairs={{0,1},{1,0},{2,3},{3,2},{4,5},{5,4},{6,7},{7,6},{8,9},{9,8},{10,11... | collective-permute-start | bytes 294920 | tf_op jit(solution)/shard_map/ppermute | solution.py:123

commit v5 on v4

--- a/solution.py
+++ b/solution.py
@@ -31,31 +31,45 @@
     blocks, each, _ = cols_ref.shape
     pieces, _, block = own_hbm.shape
     chromosomes, groups = counts_ref.shape[0], sum_ref.shape[0]
-    fetch = pltpu.make_async_copy(cols_hbm, cols_ref, col_sem)
-    copies = []
+    parts = col_sem.shape[0]
+    run = blocks // parts
+    fetches = [
+        pltpu.make_async_copy(
+            cols_hbm.at[k * run : (k + 1) * run], cols_ref.at[k * run : (k + 1) * run], col_sem.at[k]
+        )
+        for k in range(parts)
+    ]
+    tails, wholes = [], []
     for h, hbm in enumerate((own_hbm, other_hbm)):
         half = me_ref[1] if h == 0 else 1 - me_ref[1]
         for k in range(pieces):
             spot = pl.ds(pl.multiple_of((2 * k + half) * block, block), block)
-            copies.append((hbm.at[k, rows : rows + 16, :], tail_ref.at[:, spot]))
-            copies.append((hbm.at[k, 0:rows, :], rows_ref.at[:, spot]))
-    copies = [
-        pltpu.make_async_copy(source, target, row_sem.at[i])
-        for i, (source, target) in enumerate(copies)
-    ]
-    for copy in copies:
+            i = 2 * (h * pieces + k)
+            tails.append(
+                pltpu.make_async_copy(
+                    hbm.at[k, rows : rows + 16, :], tail_ref.at[:, spot], row_sem.at[i]
+                )
+            )
+            wholes.append(
+                pltpu.make_async_copy(
+                    hbm.at[k, 0:rows, :], rows_ref.at[:, spot], row_sem.at[i + 1]
+                )
+            )
+    for copy in tails + fetches + wholes:
         copy.start()
-    fetch.start()
-    for copy in copies:
+    for copy in tails:
         copy.wait()
     tail = tail_ref[...].astype(F32)
     twice = 2.0 * (tail[0:1] + tail[1:2])
     spread = twice * (1.0 - 0.5 * twice)
     lane = lax.broadcasted_iota(jnp.int32, (1, variants), 1)
-    fetch.wait()
     for k in range(blocks):
+        if k % run == 0:
+            fetches[k // run].wait()
         codes = cols_ref[k, :, 0:variants].astype(F32)
         z_ref[k * each : (k + 1) * each, :] = (codes - twice).astype(BF16)
+    for copy in wholes:
+        copy.wait()
     for a, (first, end, start) in enumerate(segments(counts_ref, variants)):
         member = (lane >= first) & (lane < end)
         denominator = jnp.sum(jnp.where(member, spread, 0.0), axis=1, keepdims=True)
@@ -66,7 +80,7 @@
             window, z_ref[:, pl.ds(start, WINDOW)], NT, preferred_element_type=F32
         ) * (1.0 / denominator)
     pairs = [[mask_ref[a, b].astype(F32) for b in range(chromosomes)] for a in range(chromosomes)]
-    high = 16
+    high = 32
 
     @pl.loop(0, rows // high)
     def _(i):
@@ -111,7 +125,7 @@
             pltpu.VMEM((chromosomes, rows, columns), BF16),
             pltpu.VMEM((groups, rows, samples), F32),
             pltpu.SemaphoreType.DMA((4 * pieces,)),
-            pltpu.SemaphoreType.DMA,
+            pltpu.SemaphoreType.DMA((4,)),
         ],
         compiler_params=pltpu.CompilerParams(vmem_limit_bytes=30 << 20),
         name="apply",

time: 81.7 us -> 81.8 us (level)
  no operation moved by 1% of the time
where the time goes in v5:
time: 81.8 us; the launch traced here: 81.4 us
  blocking collectives  33.7 us (41%)
  starting transfers between devices  24.5 us (30%)
  Pallas kernels  9.45 us (12%)
  waiting for transfers between devices  9.2 us (11%)
  other arithmetic  2.65 us (3%)
  local copies, waits for them, and re-layouts  1.7 us (2%)
    all_to_all x1, blocking collectives, body(): mine = lax.all_to_all(codes, ('c', 'l'), 0, 0, tiled=True)  17 us
    all_gather x1, blocking collectives, body(): own = lax.all_gather(local, 'c', axis=0, tiled=False)  16.7 us
    ppermute x3, starting transfers between devices, shifted(): return lax.ppermute(x, axis, [(i, (i + k) % n) for i in range(n)])  12.1 us
    pallas_call x1, Pallas kernels, apply(): pl.pallas_call(apply_kernel, out_shape=[jax.ShapeDtypeStruct((groups // 2...  9.45 us
    all_to_all x1, starting transfers between devices, body(): lax.all_to_all(jnp.broadcast_to(held[None], (plane, *held.shape)), ('y',...  6.9 us
    ppermute x1, starting transfers between devices, body(): second = lax.ppermute(chip[1], ('c', 'v'), last)  5.46 us
    ppermute x3, waiting for transfers between devices, shifted(): return lax.ppermute(x, axis, [(i, (i + k) % n) for i in range(n)])  4.03 us
    all_to_all x1, waiting for transfers between devices, body(): lax.all_to_all(jnp.broadcast_to(held[None], (plane, *held.shape)), ('y',...  2.5 us
  transfers between devices with their start and end apart: 6, of which 6 were waited for; matrix products, arithmetic and copies ran while one was open for 0% of the time, Pallas kernels for 0%

profile of v5, /device:TPU:1, one launch (start us, length us, event | category | flops | bytes accessed | tf_op | source)
XLA Modules:
  0.0 81.4 jit_solution(9348222858316318326)
XLA Ops:
  0.0 0.9 %convert_element_type.39 = bf16[64,512]{1,0:T(8,128)(2,1)S(1)} convert(s32[64,512]{1,0:T(8,128)} %param.8) | non-fusion elementwise | flops 32768 | bytes 196608 | tf_op jit(solution)/shard_map/convert_element_type | solution.py:146
  0.9 0.7 pad_maximum_fusion
  1.7 17.0 %all_to_all.10 = bf16[8,16,640]{2,1,0:T(8,128)(2,1)S(1)} all-to-all(bf16[8,16,640]{2,1,0:T(8,128)(2,1)S(1)} %bitcast.22), channel_id=1, replica_groups=mesh['c'=4,'y'=4,'x'=4,'l'=2,'v'=2] {'c','l'}, dimensions={0} | all-to-all | bytes 327680 | tf_op jit(solution)/shard_map/all_to_all | solution.py:150
  18.7 1.5 %broadcast_in_dim.35 = bf16[16,32,2176]{2,1,0:T(8,128)(2,1)} broadcast(bf16[32,2176]{1,0:T(8,128)(2,1)S(1)} %bitcast.26), dimensions={1,2} | broadcast | bytes 2367488 | tf_op jit(solution)/shard_map/broadcast_in_dim | solution.py:157
  20.2 0.0 copy-start.4
  20.2 0.0 copy-start.3
  20.2 0.0 copy-start.1
  20.2 0.0 copy-start.2
  20.3 6.9 %all-to-all-start.1 = ((bf16[16,32,2176]{2,1,0:T(8,128)(2,1)}), bf16[16,32,2176]{2,1,0:T(8,128)(2,1)S(1)}, u32[]{:S(2)}, u32[]{:S(2)}) async-start(bf16[16,32,2176]{2,1,0:T(8,128)(2,1)} %broadcast_in_dim.35), calls=%async_computation.1 | async-start | bytes 4456448 | tf_op jit(solution)/shard_map/all_to_all | solution.py:156
  27.2 0.0 copy-done.4
  27.2 0.1 pad.5.clone
  27.3 0.0 copy-done.3
  27.3 0.1 maximum_maximum_fusion
  27.5 16.7 %all-gather = bf16[1600,256]{1,0:T(8,128)(2,1)S(1)} all-gather(bf16[400,256]{1,0:T(8,128)(2,1)S(1)} %maximum_maximum_fusion), channel_id=2, replica_groups=mesh['c'=4,'y'=4,'x'=4,'l'=2,'v'=2] {'c'}, dimensions={0}, use_global_device_ids=true | all-gather | bytes 1024000 | tf_op jit(solution)/shard_map/all_gather | solution.py:168
  44.2 5.1 %collective-permute-start = (bf16[4,400,256]{2,1,0:T(8,128)(2,1)S(1)}, bf16[4,400,256]{2,1,0:T(8,128)(2,1)}, u32[]{:S(2)}, u32[]{:S(2)}) collective-permute-start(bf16[4,400,256]{2,1,0:T(8,128)(2,1)S(1)} %bitcast.20), channel_id=1, source_target_pairs={{0,1},{1,0},{2,3},{3,2},{4,5},{5,4},{6,7},{7,6},{8,9},{9,8},{10,11... | collective-permute-start | bytes 2457608 | tf_op jit(solution)/shard_map/ppermute | solution.py:137
  49.3 0.1 pad_add_fusion.me_ref
  49.4 2.0 %collective-permute-done.other_hbm = bf16[4,400,256]{2,1,0:T(8,128)(2,1)} collective-permute-done((bf16[4,400,256]{2,1,0:T(8,128)(2,1)S(1)}, bf16[4,400,256]{2,1,0:T(8,128)(2,1)}, u32[]{:S(2)}, u32[]{:S(2)}) %collective-permute-start) | collective-permute-done | bytes 819232 | tf_op jit(solution)/shard_map/ppermute | solution.py:137
  51.4 2.5 %all-to-all-done.1.cols_hbm = bf16[16,32,2176]{2,1,0:T(8,128)(2,1)S(1)} async-done(((bf16[16,32,2176]{2,1,0:T(8,128)(2,1)}), bf16[16,32,2176]{2,1,0:T(8,128)(2,1)S(1)}, u32[]{:S(2)}, u32[]{:S(2)}) %all-to-all-start.1) | async-done | bytes 2228256 | tf_op jit(solution)/shard_map/all_to_all | solution.py:156
  53.9 0.0 copy-done
  53.9 0.0 copy-done.1
  53.9 0.0 copy-done.2
  53.9 9.5 %apply.1 = (bf16[2,384,128]{2,1,0:T(8,128)(2,1)S(1)}, bf16[2,384,128]{2,1,0:T(8,128)(2,1)S(1)}) custom-call(s32[2]{0:T(128)S(1)} %pad_add_fusion.me_ref, s32[8]{0:T(128)S(1)} %copy-done.1, s32[8]{0:T(128)S(1)} %copy-done.2, s32[8,8]{1,0:T(8,128)S(1)} %copy-done, bf16[4,400,256]{2,1,0:T(8,128)(2,1)S(1)} %bitcast.21, ...), custom_call_target="tpu_custom_call" | custom-call | tf_op jit(solution)/shard_map/apply/pallas_call | solution.py:114
  63.3 6.2 %collective-permute-start.1 = (bf16[2,384,128]{2,1,0:T(8,128)(2,1)S(1)}, bf16[2,384,128]{2,1,0:T(8,128)(2,1)S(1)}, u32[]{:S(2)}, u32[]{:S(2)}) collective-permute-start(bf16[2,384,128]{2,1,0:T(8,128)(2,1)S(1)} %get-tuple-element.8), channel_id=1, source_target_pairs={{0,1},{1,0},{2,3},{3,2},{4,5},{5,4},{6,7},{7,6},{8,9},{9,8},{10,11... | collective-permute-start | bytes 589832 | tf_op jit(solution)/shard_map/ppermute | solution.py:137
  69.5 1.1 %collective-permute-done.1 = bf16[2,384,128]{2,1,0:T(8,128)(2,1)S(1)} collective-permute-done((bf16[2,384,128]{2,1,0:T(8,128)(2,1)S(1)}, bf16[2,384,128]{2,1,0:T(8,128)(2,1)S(1)}, u32[]{:S(2)}, u32[]{:S(2)}) %collective-permute-start.1) | collective-permute-done | bytes 196640 | tf_op jit(solution)/shard_map/ppermute | solution.py:137
  70.6 0.1 add_convert_fusion
  70.7 0.1 collective-permute-start.2
  70.8 5.5 %collective-permute-start.3 = (bf16[384,128]{1,0:T(8,128)(2,1)S(1)}, bf16[384,128]{1,0:T(8,128)(2,1)S(1)}, u32[]{:S(2)}, u32[]{:S(2)}) collective-permute-start(bf16[384,128]{1,0:T(8,128)(2,1)S(1)} %get-tuple-element.9), channel_id=1, source_target_pairs={{1,193},{65,1},{129,65},{193,129},{3,195},{67,3},{131,67},{195,131... | collective-permute-start | bytes 294920 | tf_op jit(solution)/shard_map/ppermute | solution.py:178
  76.2 0.9 %collective-permute-done.2 = bf16[384,128]{1,0:T(8,128)(2,1)S(1)} collective-permute-done((bf16[384,128]{1,0:T(8,128)(2,1)S(1)}, bf16[384,128]{1,0:T(8,128)(2,1)S(1)}, u32[]{:S(2)}, u32[]{:S(2)}) %collective-permute-start.2) | collective-permute-done | bytes 98336 | tf_op jit(solution)/shard_map/ppermute | solution.py:177
  77.2 1.7 %collective-permute-done.3 = bf16[384,128]{1,0:T(8,128)(2,1)S(1)} collective-permute-done((bf16[384,128]{1,0:T(8,128)(2,1)S(1)}, bf16[384,128]{1,0:T(8,128)(2,1)S(1)}, u32[]{:S(2)}, u32[]{:S(2)}) %collective-permute-start.3) | collective-permute-done | bytes 98336 | tf_op jit(solution)/shard_map/ppermute | solution.py:178
  78.9 0.8 %collective-permute-start.4 = (bf16[384,128]{1,0:T(8,128)(2,1)S(1)}, bf16[384,128]{1,0:T(8,128)(2,1)S(1)}, u32[]{:S(2)}, u32[]{:S(2)}) collective-permute-start(bf16[384,128]{1,0:T(8,128)(2,1)S(1)} %add_convert_fusion.2), channel_id=1, source_target_pairs={{0,1},{1,0},{2,3},{3,2},{4,5},{5,4},{6,7},{7,6},{8,9},{9,8},{10,11... | collective-permute-start | bytes 294920 | tf_op jit(solution)/shard_map/ppermute | solution.py:137
  79.8 0.9 %collective-permute-done.4 = bf16[384,128]{1,0:T(8,128)(2,1)S(1)} collective-permute-done((bf16[384,128]{1,0:T(8,128)(2,1)S(1)}, bf16[384,128]{1,0:T(8,128)(2,1)S(1)}, u32[]{:S(2)}, u32[]{:S(2)}) %collective-permute-start.4) | collective-permute-done | bytes 98336 | tf_op jit(solution)/shard_map/ppermute | solution.py:137
  80.7 0.7 fusion
  (16 shorter events, 0.2 us)
Async XLA Ops:
  20.2 6.9 %copy-start.4 = (f32[256]{0:T(256)S(1)}, f32[256]{0:T(256)}, u32[]{:S(2)}) copy-start(f32[256]{0:T(256)} %param.9) | copy-start | bytes 3076
  20.2 7.1 %copy-start.3 = (s32[384,256]{1,0:T(8,128)S(1)}, s32[384,256]{1,0:T(8,128)}, u32[]{:S(2)}) copy-start(s32[384,256]{1,0:T(8,128)} %param.7) | copy-start | bytes 1179652
  20.2 33.6 %copy-start = (s32[8,8]{1,0:T(8,128)S(1)}, s32[8,8]{1,0:T(8,128)}, u32[]{:S(2)}) copy-start(s32[8,8]{1,0:T(8,128)} %mask_ref.1) | copy-start | bytes 772
  20.2 33.6 %copy-start.1 = (s32[8]{0:T(128)S(1)}, s32[8]{0:T(128)}, u32[]{:S(2)}) copy-start(s32[8]{0:T(128)} %counts_ref.1) | copy-start | bytes 100
  20.2 33.6 %copy-start.2 = (s32[8]{0:T(128)S(1)}, s32[8]{0:T(128)}, u32[]{:S(2)}) copy-start(s32[8]{0:T(128)} %group_ref.1) | copy-start | bytes 100
  20.3 33.6 %all-to-all-start.1 = ((bf16[16,32,2176]{2,1,0:T(8,128)(2,1)}), bf16[16,32,2176]{2,1,0:T(8,128)(2,1)S(1)}, u32[]{:S(2)}, u32[]{:S(2)}) async-start(bf16[16,32,2176]{2,1,0:T(8,128)(2,1)} %broadcast_in_dim.35), calls=%async_computation.1 | async-start | bytes 4456448 | tf_op jit(solution)/shard_map/all_to_all | solution.py:156
  44.2 7.2 %collective-permute-start = (bf16[4,400,256]{2,1,0:T(8,128)(2,1)S(1)}, bf16[4,400,256]{2,1,0:T(8,128)(2,1)}, u32[]{:S(2)}, u32[]{:S(2)}) collective-permute-start(bf16[4,400,256]{2,1,0:T(8,128)(2,1)S(1)} %bitcast.20), channel_id=1, source_target_pairs={{0,1},{1,0},{2,3},{3,2},{4,5},{5,4},{6,7},{7,6},{8,9},{9,8},{10,11... | collective-permute-start | bytes 2457608 | tf_op jit(solution)/shard_map/ppermute | solution.py:137
  63.3 7.2 %collective-permute-start.1 = (bf16[2,384,128]{2,1,0:T(8,128)(2,1)S(1)}, bf16[2,384,128]{2,1,0:T(8,128)(2,1)S(1)}, u32[]{:S(2)}, u32[]{:S(2)}) collective-permute-start(bf16[2,384,128]{2,1,0:T(8,128)(2,1)S(1)} %get-tuple-element.8), channel_id=1, source_target_pairs={{0,1},{1,0},{2,3},{3,2},{4,5},{5,4},{6,7},{7,6},{8,9},{9,8},{10,11... | collective-permute-start | bytes 589832 | tf_op jit(solution)/shard_map/ppermute | solution.py:137
  70.7 6.5 %collective-permute-start.2 = (bf16[384,128]{1,0:T(8,128)(2,1)S(1)}, bf16[384,128]{1,0:T(8,128)(2,1)S(1)}, u32[]{:S(2)}, u32[]{:S(2)}) collective-permute-start(bf16[384,128]{1,0:T(8,128)(2,1)S(1)} %get-tuple-element.10), channel_id=1, source_target_pairs={{0,128},{64,192},{128,0},{192,64},{1,65},{65,129},{129,193},{193,1... | collective-permute-start | bytes 294920 | tf_op jit(solution)/shard_map/ppermute | solution.py:177
  70.8 8.1 %collective-permute-start.3 = (bf16[384,128]{1,0:T(8,128)(2,1)S(1)}, bf16[384,128]{1,0:T(8,128)(2,1)S(1)}, u32[]{:S(2)}, u32[]{:S(2)}) collective-permute-start(bf16[384,128]{1,0:T(8,128)(2,1)S(1)} %get-tuple-element.9), channel_id=1, source_target_pairs={{1,193},{65,1},{129,65},{193,129},{3,195},{67,3},{131,67},{195,131... | collective-permute-start | bytes 294920 | tf_op jit(solution)/shard_map/ppermute | solution.py:178
  78.9 1.8 %collective-permute-start.4 = (bf16[384,128]{1,0:T(8,128)(2,1)S(1)}, bf16[384,128]{1,0:T(8,128)(2,1)S(1)}, u32[]{:S(2)}, u32[]{:S(2)}) collective-permute-start(bf16[384,128]{1,0:T(8,128)(2,1)S(1)} %add_convert_fusion.2), channel_id=1, source_target_pairs={{0,1},{1,0},{2,3},{3,2},{4,5},{5,4},{6,7},{7,6},{8,9},{9,8},{10,11... | collective-permute-start | bytes 294920 | tf_op jit(solution)/shard_map/ppermute | solution.py:137
